TPU v7x, 128 devices: a whole 4x4x4 slice. The times are simulated.
128 devices in a mesh: dp: 8 (over x, core), expert: 16 (over y, z).
Axes of the slice: x: 4, y: 4, z: 4, core: 2. Of those that a mesh axis runs over, the one named last changes fastest.
Arguments:
- upper_half: bfloat16 [16384, 2048], P(('dp', 'expert')), may hold values from -6 to 6
- lower_half: bfloat16 [16384, 2048], P(('dp', 'expert')), may hold values from -6 to 6
- upper_grad: bfloat16 [16384, 2048], P(('dp', 'expert')), may hold values from -6 to 6
- lower_grad: bfloat16 [16384, 2048], P(('dp', 'expert')), may hold values from -3 to 3
- expert_ids: int32 [16384, 6], P(('dp', 'expert')), may hold values from 0 to 31, as said below
- gate_weights: int32 [16384, 6], P(('dp', 'expert')), may hold values from 64 to 383
- route_slots: int32 [16384, 6], P(('dp', 'expert')), may hold values from 0 to 30, as said below
- expert_weight: bfloat16 [32, 2048, 2304], P('expert'), may hold values from -0.15625 to 0.15625
Outputs:
- upper_input: bfloat16 [16384, 2048], P(('dp', 'expert'))
- lower_input_grad: bfloat16 [16384, 2048], P(('dp', 'expert'))
- weight_grad: float32 [32, 2048, 2304], P('expert', 'dp')
Inputs may be any that keep to these rules, and one draw needn't show every extreme that they name: `expert_ids`: each row names 6 different experts. `route_slots`: A route is live when its slot is below 30; a slot of 30 marks a route dropped for lack of room. Among the rows of one device, the live routes to one expert hold distinct slots. In every draw some expert has all 30 slots live from every device, and some route is dropped.
All inputs are finite; a program needn't handle non-finite values.
Results may differ from a plain program's by a relative error of at most 0.015.
Values may be sent and summed in bfloat16 or wider, within the bound.
A program may use at most 192 MiB of HBM per device.

v0:
```python
import jax
import jax.numpy as jnp
from jax import lax
from jax.sharding import PartitionSpec as P

GATE_DENOM = 1024


norm_eps = 1e-06


def scatter_rows(values, flat_index, slots_total):
    buffer = jnp.zeros((slots_total, values.shape[-1]), values.dtype)
    return buffer.at[flat_index].set(values, mode="drop")


def expert_forward(normed_rows, expert_weight, hidden_width):
    gate_up = jnp.einsum(
        "sjcd,jdf->sjcf",
        normed_rows,
        expert_weight[:, :, : 2 * hidden_width],
        preferred_element_type=jnp.float32,
    )
    gate_part = gate_up[..., :hidden_width]
    up_part = gate_up[..., hidden_width:]
    sigmoid_gate = jax.nn.sigmoid(gate_part)
    hidden = (gate_part * sigmoid_gate * up_part).astype(jnp.bfloat16)
    output = jnp.einsum(
        "sjch,jdh->sjcd",
        hidden,
        expert_weight[:, :, 2 * hidden_width :],
        preferred_element_type=jnp.float32,
    ).astype(jnp.bfloat16)
    return (gate_up, hidden, output)


def expert_backward(gate_up, scaled_rows, expert_weight, hidden_width):
    gate_part = gate_up[..., :hidden_width]
    up_part = gate_up[..., hidden_width:]
    sigmoid_gate = jax.nn.sigmoid(gate_part)
    grad_hidden = jnp.einsum(
        "sjcd,jdh->sjch",
        scaled_rows,
        expert_weight[:, :, 2 * hidden_width :],
        preferred_element_type=jnp.float32,
    )
    grad_gate = grad_hidden * up_part * sigmoid_gate * (1.0 + gate_part * (1.0 - sigmoid_gate))
    grad_up = grad_hidden * gate_part * sigmoid_gate
    grad_gate_up = jnp.concatenate([grad_gate, grad_up], axis=-1).astype(jnp.bfloat16)
    grad_input = jnp.einsum(
        "sjcf,jdf->sjcd",
        grad_gate_up,
        expert_weight[:, :, : 2 * hidden_width],
        preferred_element_type=jnp.float32,
    ).astype(jnp.bfloat16)
    return (grad_gate_up, grad_input)


def term_maker(normed_flat, grad_flat, scaled_flat, hidden_flat):

    def weight_term(offset, amount):
        upper_block = lax.dot_general(
            normed_flat, grad_flat, (((0,), (0,)), ((), ())), preferred_element_type=jnp.float32
        )
        lower_block = lax.dot_general(
            scaled_flat, hidden_flat, (((0,), (0,)), ((), ())), preferred_element_type=jnp.float32
        )
        return jnp.concatenate([upper_block, lower_block], axis=1)

    return weight_term


def shards(
    upper_half,
    lower_half,
    upper_grad,
    lower_grad,
    expert_ids,
    gate_weights,
    route_slots,
    expert_weight,
):
    row_count = upper_half.shape[0]
    model_width = upper_half.shape[1]
    local_experts = expert_weight.shape[0]
    hidden_width = expert_weight.shape[2] // 3
    peer_count = lax.axis_size("expert")
    expert_count = local_experts * peer_count
    top_routes = expert_ids.shape[1]
    capacity = 5 * row_count * top_routes // (4 * expert_count)
    slots_total = expert_count * capacity
    kept_routes = route_slots < capacity
    flat_index = jnp.where(kept_routes, expert_ids * capacity + route_slots, slots_total)
    route_index = flat_index.reshape(-1)
    lower_float = lower_half.astype(jnp.float32)
    norm_scale = lax.rsqrt(jnp.mean(lower_float * lower_float, axis=1, keepdims=True) + norm_eps)
    normed = (lower_float * norm_scale).astype(jnp.bfloat16)
    shares = gate_weights.astype(jnp.float32) / GATE_DENOM
    scaled = (shares[:, :, None] * upper_grad.astype(jnp.float32)[:, None, :]).astype(jnp.bfloat16)
    repeated = jnp.broadcast_to(normed[:, None, :], (row_count, top_routes, model_width)).reshape(
        -1, model_width
    )
    send_shape = (peer_count, local_experts, capacity, model_width)
    normed_send = scatter_rows(repeated, route_index, slots_total).reshape(send_shape)
    scaled_send = scatter_rows(scaled.reshape(-1, model_width), route_index, slots_total).reshape(
        send_shape
    )
    received = lax.all_to_all(normed_send, "expert", split_axis=0, concat_axis=0, tiled=True)
    gate_part_up, hidden_part, output = expert_forward(received, expert_weight, hidden_width)
    returned = lax.all_to_all(output, "expert", split_axis=0, concat_axis=0, tiled=True)
    scaled_rows = lax.all_to_all(scaled_send, "expert", split_axis=0, concat_axis=0, tiled=True)
    grad_gate_up, grad_input = expert_backward(
        gate_part_up, scaled_rows, expert_weight, hidden_width
    )
    input_back = lax.all_to_all(grad_input, "expert", split_axis=0, concat_axis=0, tiled=True)
    output_flat = returned.reshape(slots_total, model_width)
    input_flat = input_back.reshape(slots_total, model_width)
    gathered = jnp.take(output_flat, flat_index, axis=0, mode="fill", fill_value=0)
    mixture = jnp.sum(shares[:, :, None] * gathered.astype(jnp.float32), axis=1)
    upper_input = (upper_half.astype(jnp.float32) - mixture).astype(jnp.bfloat16)
    grad_gathered = jnp.take(input_flat, flat_index, axis=0, mode="fill", fill_value=0)
    grad_normed = jnp.sum(grad_gathered.astype(jnp.float32), axis=1)
    inner_mean = jnp.mean(lower_float * grad_normed, axis=1, keepdims=True)
    cubed = norm_scale * norm_scale * norm_scale
    lower_input_grad = (
        lower_grad.astype(jnp.float32) + norm_scale * grad_normed - lower_float * cubed * inner_mean
    ).astype(jnp.bfloat16)
    share_rows = model_width // lax.axis_size("dp")
    partials = []
    for column in range(local_experts):
        weight_term = term_maker(
            received[:, column].reshape(-1, model_width),
            grad_gate_up[:, column].reshape(-1, 2 * hidden_width),
            scaled_rows[:, column].reshape(-1, model_width),
            hidden_part[:, column].reshape(-1, hidden_width),
        )
        partials.append(
            lax.psum_scatter(
                weight_term(jnp.int32(0), lax.axis_size("dp") * share_rows).astype(jnp.bfloat16),
                "dp",
                scatter_dimension=0,
                tiled=True,
            ).astype(jnp.float32)
        )
    weight_grad = jnp.stack(partials)
    return (upper_input, lower_input_grad, weight_grad)


def solution(mesh):
    in_specs = (
        P(("dp", "expert"), None),
        P(("dp", "expert"), None),
        P(("dp", "expert"), None),
        P(("dp", "expert"), None),
        P(("dp", "expert"), None),
        P(("dp", "expert"), None),
        P(("dp", "expert"), None),
        P("expert", None, None),
    )
    out_specs = (P(("dp", "expert"), None), P(("dp", "expert"), None), P("expert", "dp", None))
    return jax.shard_map(shards, mesh=mesh, in_specs=in_specs, out_specs=out_specs, check_vma=False)
```

profile of v0, /device:TPU:0, one launch (start us, length us, event | category | flops | bytes accessed | tf_op | source)
XLA Modules:
  0.0 414.2 jit_solution(10004560071038294433)
XLA Ops:
  7.2 0.7 convert_multiply_fusion.4
  7.9 0.1 copy.27
  8.0 0.1 mul.113
  8.1 0.7 compare_and_fusion
  8.8 0.1 copy.29
  8.9 0.1 reshape.105
  9.1 5.3 %mul.115 = f32[128,6,2048]{2,1,0:T(8,128)} broadcast(bf16[128,2048]{1,0:T(8,128)(2,1)} %param.12), dimensions={0,2} | broadcast | bytes 6815744 | tf_op jit(solution)/shard_map/mul | solution.py:99
  14.4 8.2 %mul.116 = f32[768,2048]{1,0:T(8,128)} reshape(f32[128,6,2048]{2,1,0:T(8,128)} %mul.115) | data formatting | bytes 12582912 | tf_op jit(solution)/shard_map/mul | solution.py:99
  22.7 14.8 %scatter_custom_fusion.1 = bf16[960,2048]{1,0:T(8,128)(2,1)} fusion(s32[768]{0:T(1024)S(1)} %fusion.41, f32[768,2048]{1,0:T(8,128)} %mul.116, f32[768]{0:T(1024)S(1)} %mul.113, bf16[]{:T(256)} %constant.5.clone.1), kind=kCustom, calls=%fused_computation.33 | custom fusion | flops 3145728 | bytes 10227714 | tf_op jit(solution)/shard_map/scatter | solution.py:14
  37.5 5.0 %reshape.109 = bf16[16,2,30,2048]{3,2,1,0:T(8,128)(2,1)} reshape(bf16[960,2048]{1,0:T(8,128)(2,1)} %scatter_custom_fusion.1) | data formatting | bytes 7864320 | tf_op jit(solution)/shard_map/reshape | solution.py:105
  42.5 8.2 %copy.37 = bf16[16,2,30,2048]{3,1,2,0:T(2,128)(2,1)} copy(bf16[16,2,30,2048]{3,2,1,0:T(8,128)(2,1)} %reshape.109) | data formatting | bytes 7864320 | tf_op jit(solution)/shard_map/reshape | solution.py:105
  50.7 8.3 %all-to-all-start.2 = ((bf16[16,2,30,2048]{3,1,2,0:T(2,128)(2,1)}), bf16[16,2,30,2048]{3,1,2,0:T(2,128)(2,1)}, u32[]{:S(2)}, u32[]{:S(2)}) async-start(bf16[16,2,30,2048]{3,1,2,0:T(2,128)(2,1)} %copy.37), calls=%async_computation.2 | async-start | bytes 7864320 | tf_op jit(solution)/shard_map/all_to_all | solution.py:111
  59.0 0.2 fusion.35
  59.2 0.2 fusion.36
  59.4 2.7 broadcast_in_dim.13
  62.1 4.9 %reshape.139 = bf16[768,2048]{1,0:T(8,128)(2,1)S(1)} reshape(bf16[128,6,2048]{2,1,0:T(8,128)(2,1)} %broadcast_in_dim.13) | data formatting | bytes 6291456 | tf_op jit(solution)/shard_map/reshape | solution.py:100
  66.9 9.5 %scatter_custom_fusion = bf16[960,2048]{1,0:T(8,128)(2,1)} fusion(s32[768]{0:T(1024)S(1)} %fusion.41, bf16[768,2048]{1,0:T(8,128)(2,1)S(1)} %reshape.139, bf16[]{:T(256)} %constant.5.clone.1), kind=kCustom, calls=%fused_computation.50 | custom fusion | bytes 3932162 | tf_op jit(solution)/shard_map/scatter | solution.py:14
  76.4 5.0 %reshape.107 = bf16[16,2,30,2048]{3,2,1,0:T(8,128)(2,1)} reshape(bf16[960,2048]{1,0:T(8,128)(2,1)} %scatter_custom_fusion) | data formatting | bytes 7864320 | tf_op jit(solution)/shard_map/reshape | solution.py:104
  81.5 8.2 %copy.30 = bf16[16,2,30,2048]{3,1,2,0:T(2,128)(2,1)} copy(bf16[16,2,30,2048]{3,2,1,0:T(8,128)(2,1)} %reshape.107) | data formatting | bytes 7864320 | tf_op jit(solution)/shard_map/reshape | solution.py:104
  89.7 26.8 %all-to-all-done.2 = bf16[16,2,30,2048]{3,1,2,0:T(2,128)(2,1)} async-done(((bf16[16,2,30,2048]{3,1,2,0:T(2,128)(2,1)}), bf16[16,2,30,2048]{3,1,2,0:T(2,128)(2,1)}, u32[]{:S(2)}, u32[]{:S(2)}) %all-to-all-start.2) | async-done | bytes 3932192 | tf_op jit(solution)/shard_map/all_to_all | solution.py:111
  116.5 10.5 %all-to-all-start = ((bf16[16,2,30,2048]{3,1,2,0:T(2,128)(2,1)}), bf16[16,2,30,2048]{3,1,2,0:T(2,128)(2,1)}, u32[]{:S(2)}, u32[]{:S(2)}) async-start(bf16[16,2,30,2048]{3,1,2,0:T(2,128)(2,1)} %copy.30), calls=%async_computation | async-start | bytes 7864320 | tf_op jit(solution)/shard_map/all_to_all | solution.py:108
  127.0 0.0 reduce-scatter.3.cloned.1.call-start
  127.0 6.0 %copy.38 = bf16[16,2,30,2048]{3,2,0,1:T(8,128)(2,1)} copy(bf16[16,2,30,2048]{3,1,2,0:T(2,128)(2,1)} %all-to-all-done.2) | data formatting | bytes 7864320 | tf_op jit(solution)/shard_map/all_to_all | solution.py:111
  133.0 44.5 %all-to-all-done = bf16[16,2,30,2048]{3,1,2,0:T(2,128)(2,1)} async-done(((bf16[16,2,30,2048]{3,1,2,0:T(2,128)(2,1)}), bf16[16,2,30,2048]{3,1,2,0:T(2,128)(2,1)}, u32[]{:S(2)}, u32[]{:S(2)}) %all-to-all-start) | async-done | bytes 3932192 | tf_op jit(solution)/shard_map/all_to_all | solution.py:108
  177.5 15.3 %fusion.12 = f32[16,2,30,1536]{3,2,0,1:T(8,128)S(1)} fusion(bf16[2,2048,2304]{2,1,0:T(8,128)(2,1)} %param.17, bf16[16,2,30,2048]{3,1,2,0:T(2,128)(2,1)} %all-to-all-done), kind=kOutput, calls=%fused_computation.25 | convolution fusion | flops 6039797760 | bytes 22413312 | tf_op jit(solution)/shard_map/sjcd,jdf->sjcf/dot_general | solution.py:18
  192.8 0.0 copy-start.2
  192.8 9.3 %fusion.22 = (bf16[16,2,30,768]{3,2,0,1:T(8,128)(2,1)S(1)}, bf16[16,2,30,768]{3,2,0,1:T(8,128)(2,1)S(1)}, bf16[16,2,30,768]{3,2,0,1:T(8,128)(2,1)S(1)}) fusion(f32[16,2,30,1536]{3,2,0,1:T(8,128)S(1)} %fusion.12, bf16[2,2048,2304]{2,1,0:T(8,128)(2,1)} %param.17, bf16[16,2,30,2048]{3,1,2,0:T(2,128)(2,1)} %all-to-all-done.2), kind=kOutput, calls=%fused_computation.38 | convolution fusion | flops 3031695360 | bytes 20545536 | tf_op jit(solution)/shard_map/sjcd,jdh->sjch/dot_general | solution.py:41
  202.1 0.0 copy-start.9
  202.1 0.0 copy-done.2
  202.1 1.9 bitcast_convert_fusion.3
  204.0 3.9 copy.31
  208.0 3.8 bitcast_convert_fusion.1
  211.8 11.7 %pad_maximum_fusion = bf16[2048,2304]{0,1:T(8,128)(2,1)} fusion(bf16[2048,768]{0,1:T(8,128)(2,1)S(1)} %bitcast_convert_fusion.3, bf16[2048,1536]{0,1:T(8,128)(2,1)S(1)} %bitcast_convert_fusion.1), kind=kLoop, calls=%fused_computation.12 | loop fusion | flops 18874368 | bytes 18874368 | tf_op jit(solution)/shard_map/concatenate | solution.py:68
  223.5 0.0 reduce-scatter.3.cloned.1.call-update
  223.5 0.0 reduce-scatter.5.cloned.1.call-start
  223.6 3.6 bitcast_convert_fusion.2
  227.2 3.8 bitcast_convert_fusion
  231.0 11.2 %pad_maximum_fusion.1 = bf16[2048,2304]{0,1:T(8,128)(2,1)} fusion(bf16[2048,768]{0,1:T(8,128)(2,1)S(1)} %bitcast_convert_fusion.2, bf16[2048,1536]{0,1:T(8,128)(2,1)S(1)} %bitcast_convert_fusion), kind=kLoop, calls=%fused_computation.13 | loop fusion | flops 18874368 | bytes 18874368 | tf_op jit(solution)/shard_map/concatenate | solution.py:68
  242.2 0.0 reduce-scatter.5.cloned.1.call-update
  242.3 6.6 %convert_bitcast_fusion.1 = bf16[16,2,30,2048]{3,2,0,1:T(8,128)(2,1)S(1)} fusion(bf16[16,2,30,768]{3,2,0,1:T(8,128)(2,1)S(1)} %get-tuple-element.19, bf16[2,2048,2304]{2,1,0:T(8,128)(2,1)} %param.17), kind=kOutput, calls=%fused_computation.27 | convolution fusion | flops 3021864960 | bytes 11698176 | tf_op jit(solution)/shard_map/sjch,jdh->sjcd/dot_general | solution.py:28
  248.9 6.0 %copy.32 = bf16[16,2,30,2048]{3,1,2,0:T(2,128)(2,1)} copy(bf16[16,2,30,2048]{3,2,0,1:T(8,128)(2,1)S(1)} %convert_bitcast_fusion.1) | data formatting | bytes 7864320 | tf_op jit(solution)/shard_map/convert_element_type | solution.py:33
  254.9 4.8 %all-to-all-start.1 = ((bf16[16,2,30,2048]{3,1,2,0:T(2,128)(2,1)}), bf16[16,2,30,2048]{3,1,2,0:T(2,128)(2,1)}, u32[]{:S(2)}, u32[]{:S(2)}) async-start(bf16[16,2,30,2048]{3,1,2,0:T(2,128)(2,1)} %copy.32), calls=%async_computation.1 | async-start | bytes 7864320 | tf_op jit(solution)/shard_map/all_to_all | solution.py:110
  259.8 9.9 %convert_bitcast_fusion = bf16[16,2,30,2048]{3,2,0,1:T(8,128)(2,1)S(1)} fusion(bf16[2,2048,2304]{2,1,0:T(8,128)(2,1)} %param.17, bf16[16,2,30,768]{3,2,0,1:T(8,128)(2,1)S(1)} %copy-done.11, bf16[16,2,30,768]{3,2,0,1:T(8,128)(2,1)S(1)} %get-tuple-element.17), kind=kOutput, calls=%fused_computation.26 | convolution fusion | flops 6047662080 | bytes 19464192 | tf_op jit(solution)/shard_map/sjcf,jdf->sjcd/dot_general | solution.py:50
  269.7 6.1 %copy.39 = bf16[16,2,30,2048]{3,1,2,0:T(2,128)(2,1)} copy(bf16[16,2,30,2048]{3,2,0,1:T(8,128)(2,1)S(1)} %convert_bitcast_fusion) | data formatting | bytes 7864320 | tf_op jit(solution)/shard_map/convert_element_type | solution.py:55
  275.7 30.0 %all-to-all-done.1 = bf16[16,2,30,2048]{3,1,2,0:T(2,128)(2,1)} async-done(((bf16[16,2,30,2048]{3,1,2,0:T(2,128)(2,1)}), bf16[16,2,30,2048]{3,1,2,0:T(2,128)(2,1)}, u32[]{:S(2)}, u32[]{:S(2)}) %all-to-all-start.1) | async-done | bytes 3932192 | tf_op jit(solution)/shard_map/all_to_all | solution.py:110
  305.7 7.2 %all-to-all-start.3 = ((bf16[16,2,30,2048]{3,1,2,0:T(2,128)(2,1)}), bf16[16,2,30,2048]{3,1,2,0:T(2,128)(2,1)}, u32[]{:S(2)}, u32[]{:S(2)}) async-start(bf16[16,2,30,2048]{3,1,2,0:T(2,128)(2,1)} %copy.39), calls=%async_computation.3 | async-start | bytes 7864320 | tf_op jit(solution)/shard_map/all_to_all | solution.py:115
  312.9 0.1 copy.28
  313.1 0.1 copy.34
  313.2 0.1 reshape.155
  313.4 6.0 %copy.33 = bf16[16,2,30,2048]{3,2,1,0:T(8,128)(2,1)} copy(bf16[16,2,30,2048]{3,1,2,0:T(2,128)(2,1)} %all-to-all-done.1) | data formatting | bytes 7864320 | tf_op jit(solution)/shard_map/all_to_all | solution.py:110
  319.4 5.1 %reshape.108 = bf16[960,2048]{1,0:T(8,128)(2,1)} reshape(bf16[16,2,30,2048]{3,2,1,0:T(8,128)(2,1)} %copy.33) | data formatting | bytes 7864320 | tf_op jit(solution)/shard_map/reshape | solution.py:116
  324.5 9.0 %gather_fusion = bf16[768,2048]{1,0:T(8,128)(2,1)S(1)} fusion(bf16[960,2048]{1,0:T(8,128)(2,1)} %reshape.108, s32[1024]{0:T(1024)S(1)} %pad_clamp_fusion), kind=kCustom, calls=%fused_computation.clone | custom fusion | bytes 6294528 | tf_op jit(solution)/shard_map/jit(_take)/gather | solution.py:118
  333.5 2.9 reshape.158
  336.4 26.6 %all-to-all-done.3 = bf16[16,2,30,2048]{3,1,2,0:T(2,128)(2,1)} async-done(((bf16[16,2,30,2048]{3,1,2,0:T(2,128)(2,1)}), bf16[16,2,30,2048]{3,1,2,0:T(2,128)(2,1)}, u32[]{:S(2)}, u32[]{:S(2)}) %all-to-all-start.3) | async-done | bytes 3932192 | tf_op jit(solution)/shard_map/all_to_all | solution.py:115
  363.0 6.0 %copy.40 = bf16[16,2,30,2048]{3,2,1,0:T(8,128)(2,1)} copy(bf16[16,2,30,2048]{3,1,2,0:T(2,128)(2,1)} %all-to-all-done.3) | data formatting | bytes 7864320 | tf_op jit(solution)/shard_map/all_to_all | solution.py:115
  369.0 5.0 %reshape.110 = bf16[960,2048]{1,0:T(8,128)(2,1)} reshape(bf16[16,2,30,2048]{3,2,1,0:T(8,128)(2,1)} %copy.40) | data formatting | bytes 7864320 | tf_op jit(solution)/shard_map/reshape | solution.py:117
  374.0 9.0 %gather_fusion.1 = bf16[768,2048]{1,0:T(8,128)(2,1)S(1)} fusion(bf16[960,2048]{1,0:T(8,128)(2,1)} %reshape.110, s32[1024]{0:T(1024)S(1)} %pad_clamp_fusion), kind=kCustom, calls=%fused_computation.1.clone | custom fusion | bytes 6294528 | tf_op jit(solution)/shard_map/jit(_take)/gather | solution.py:121
  383.0 0.0 copy-start.6
  383.0 2.8 reshape.162
  385.8 9.6 %convert_reduce_fusion = (f32[128,2048]{1,0:T(8,128)S(1)}, f32[128,2048]{1,0:T(8,128)S(1)}) fusion(bf16[128,6,2048]{2,1,0:T(8,128)(2,1)} %reshape.162, pred[128,6]{1,0:T(8,128)(4,1)S(1)} %copy.28, bf16[128,6,2048]{2,1,0:T(8,128)(2,1)} %reshape.158, f32[128,6]{1,0:T(8,128)S(1)} %copy-done.6), kind=kLoop, calls=%fused_computation.14 | loop fusion | flops 10485760 | bytes 8392448 | tf_op jit(solution)/shard_map/reduce_sum | solution.py:122
  395.4 0.2 fusion.40
  395.6 1.4 fusion.39
  397.0 4.1 maximum_convert_fusion
  401.1 6.0 %copy.46 = f32[2,256,2304]{2,1,0:T(8,128)} copy(f32[2,256,2304]{1,2,0:T(8,128)} %maximum_convert_fusion) | data formatting | bytes 9437184
  (27 shorter events, 0.1 us)
Async XLA Ops:
  8.0 6.5 %copy-start.5 = (f32[128,6]{1,0:T(8,128)}, f32[128,6]{1,0:T(8,128)S(1)}, u32[]{:S(2)}) copy-start(f32[128,6]{1,0:T(8,128)S(1)} %copy.27) | copy-start | bytes 9220
  50.7 8.3 %copy-start = (bf16[128,2048]{1,0:T(8,128)(2,1)S(1)}, bf16[128,2048]{1,0:T(8,128)(2,1)}, u32[]{:S(2)}) copy-start(bf16[128,2048]{1,0:T(8,128)(2,1)} %param.11) | copy-start | bytes 1572868
  50.7 65.8 %all-to-all-start.2 = ((bf16[16,2,30,2048]{3,1,2,0:T(2,128)(2,1)}), bf16[16,2,30,2048]{3,1,2,0:T(2,128)(2,1)}, u32[]{:S(2)}, u32[]{:S(2)}) async-start(bf16[16,2,30,2048]{3,1,2,0:T(2,128)(2,1)} %copy.37), calls=%async_computation.2 | async-start | bytes 7864320 | tf_op jit(solution)/shard_map/all_to_all | solution.py:111
  116.5 61.0 %all-to-all-start = ((bf16[16,2,30,2048]{3,1,2,0:T(2,128)(2,1)}), bf16[16,2,30,2048]{3,1,2,0:T(2,128)(2,1)}, u32[]{:S(2)}, u32[]{:S(2)}) async-start(bf16[16,2,30,2048]{3,1,2,0:T(2,128)(2,1)} %copy.30), calls=%async_computation | async-start | bytes 7864320 | tf_op jit(solution)/shard_map/all_to_all | solution.py:108
  127.0 270.0 %reduce-scatter.3.cloned.1.call-start = ((), (), s32[]{:S(2)}) async-start(), calls=%async_computation.6 | async-start | bytes 10616832 | tf_op jit(solution)/shard_map/reduce_scatter | solution.py:138
  192.8 9.3 %copy-start.2 = (bf16[16,2,30,2048]{3,2,0,1:T(8,128)(2,1)S(1)}, bf16[16,2,30,2048]{3,2,0,1:T(8,128)(2,1)}, u32[]{:S(2)}) copy-start(bf16[16,2,30,2048]{3,2,0,1:T(8,128)(2,1)} %copy.38) | copy-start | bytes 11796484
  202.1 5.9 %copy-start.9 = (bf16[16,2,30,768]{3,2,0,1:T(8,128)(2,1)}, bf16[16,2,30,768]{3,2,0,1:T(8,128)(2,1)S(1)}, u32[]{:S(2)}) copy-start(bf16[16,2,30,768]{3,2,0,1:T(8,128)(2,1)S(1)} %get-tuple-element.18) | copy-start | bytes 4423684
  208.0 3.8 copy-start.3
  223.5 173.5 %reduce-scatter.5.cloned.1.call-start = ((), (), s32[]{:S(2)}) async-start(), calls=%async_computation.7 | async-start | bytes 10616832 | tf_op jit(solution)/shard_map/reduce_scatter | solution.py:138
  223.6 3.6 copy-start.4
  223.6 3.6 copy-start.10
  254.9 4.8 %copy-start.11 = (bf16[16,2,30,768]{3,2,0,1:T(8,128)(2,1)S(1)}, bf16[16,2,30,768]{3,2,0,1:T(8,128)(2,1)}, u32[]{:S(2)}) copy-start(bf16[16,2,30,768]{3,2,0,1:T(8,128)(2,1)} %copy-done.9) | copy-start | bytes 4423684
  254.9 50.8 %all-to-all-start.1 = ((bf16[16,2,30,2048]{3,1,2,0:T(2,128)(2,1)}), bf16[16,2,30,2048]{3,1,2,0:T(2,128)(2,1)}, u32[]{:S(2)}, u32[]{:S(2)}) async-start(bf16[16,2,30,2048]{3,1,2,0:T(2,128)(2,1)} %copy.32), calls=%async_computation.1 | async-start | bytes 7864320 | tf_op jit(solution)/shard_map/all_to_all | solution.py:110
  305.7 57.3 %all-to-all-start.3 = ((bf16[16,2,30,2048]{3,1,2,0:T(2,128)(2,1)}), bf16[16,2,30,2048]{3,1,2,0:T(2,128)(2,1)}, u32[]{:S(2)}, u32[]{:S(2)}) async-start(bf16[16,2,30,2048]{3,1,2,0:T(2,128)(2,1)} %copy.39), calls=%async_computation.3 | async-start | bytes 7864320 | tf_op jit(solution)/shard_map/all_to_all | solution.py:115
  383.0 2.8 copy-start.6
  385.8 9.6 %copy-start.1 = (bf16[128,2048]{1,0:T(8,128)(2,1)S(1)}, bf16[128,2048]{1,0:T(8,128)(2,1)}, u32[]{:S(2)}) copy-start(bf16[128,2048]{1,0:T(8,128)(2,1)} %param.11) | copy-start | bytes 1572868
  385.8 9.8 %copy-start.7 = (bf16[128,2048]{1,0:T(8,128)(2,1)S(1)}, bf16[128,2048]{1,0:T(8,128)(2,1)}, u32[]{:S(2)}) copy-start(bf16[128,2048]{1,0:T(8,128)(2,1)} %param.13) | copy-start | bytes 1572868
  385.8 9.8 %copy-start.8 = (bf16[128,2048]{1,0:T(8,128)(2,1)S(1)}, bf16[128,2048]{1,0:T(8,128)(2,1)}, u32[]{:S(2)}) copy-start(bf16[128,2048]{1,0:T(8,128)(2,1)} %param.10) | copy-start | bytes 1572868
Sparse Core Ops, SparseCore 0:
  223.6 55.6 reduce-scatter.2
  281.8 57.2 reduce-scatter.4
where the time goes:
time: 422 us; the launch traced here: 414 us
  local copies, waits for them, and re-layouts  132 us (31%)
  waiting for transfers between devices  128 us (30%)
  other arithmetic  54.8 us (13%)
  matrix products  54.1 us (13%)
  starting transfers between devices  30.9 us (7%)
  between operations  14.6 us (3%)
    all_to_all x1, waiting for transfers between devices, shards(): lax.all_to_all(normed_send, 'expert', split_axis=0, concat_axis=0, tiled=...  44.5 us
    all_to_all x1, waiting for transfers between devices, shards(): lax.all_to_all(output, 'expert', split_axis=0, concat_axis=0, tiled=True)  30 us
    all_to_all x1, waiting for transfers between devices, shards(): lax.all_to_all(scaled_send, 'expert', split_axis=0, concat_axis=0, tiled=...  26.8 us
    all_to_all x1, waiting for transfers between devices, shards(): lax.all_to_all(grad_input, 'expert', split_axis=0, concat_axis=0, tiled=T...  26.6 us
    concatenate x2, other arithmetic, weight_term(): return jnp.concatenate([upper_block, lower_block], axis=1)  23 us
    dot_general x1, matrix products, expert_forward(): jnp.einsum('sjcd,jdf->sjcf', normed_rows, expert_weight[:, :, :2 * hidden...  15.3 us
    scatter x1, other arithmetic, scatter_rows(): return buffer.at[flat_index].set(values, mode='drop')  14.8 us
    mul x2, local copies, waits for them, and re-layouts, shards(): shares[:, :, None] * upper_grad.astype(jnp.float32)[:, None, :]  13.6 us
  transfers between devices with their start and end apart: 6, of which 4 were waited for; matrix products, arithmetic and copies ran while one was open for 34% of the time, Pallas kernels for 0%

commit v1 on v0

v1 whole, which is shorter than its diff:
```python
import functools

import jax
import jax.numpy as jnp
from jax import lax
from jax.experimental import pallas as pl
from jax.experimental.pallas import tpu as pltpu
from jax.sharding import PartitionSpec as P

MESH = pl.DeviceIdType.MESH
F32 = jnp.float32
BF16 = jnp.bfloat16

GATE_DENOM = 1024
NORM_EPS = 1e-06
T = 128
D = 2048
H = 768
F = 3 * H
TOPK = 6
CAP = 30
S = 32
M = 16 * S
RING = 4
SHARE = D // 8


def dot_nt(a, b):
    return lax.dot_general(a, b, (((1,), (1,)), ((), ())), preferred_element_type=F32)


def dot_tn(a, b):
    return lax.dot_general(a, b, (((0,), (0,)), ((), ())), preferred_element_type=F32)


def dot_nn(a, b):
    return lax.dot_general(a, b, (((1,), (0,)), ((), ())), preferred_element_type=F32)


def kernel(
    uh, lh, ug, lg, rt, w_hbm,
    o_up, o_lo, o_own, o_left, o_right,
    AG, RT, SD, R, O1, W, G, PX, PG, OWN, TMP, FL, FR, FT,
    ag_s, ag_r, agf_s, agf_r, rt_s, rt_r, s2_s, s2_r, rb_s, rb_r,
    px_s, px_r, pg_s, pg_r, x_s, x_r, fn_s, fn_r, loc, w_sem, credit, pcredit,
):
    dp = lax.axis_index("dp")
    ex = lax.axis_index("expert")
    x, c = dp // 2, dp % 2
    y, z = ex // RING, ex % RING
    a_me = (y, z)
    b_me = (z, y)

    def ydev(k):
        return (dp, ((y + k) % RING) * RING + z)

    def zdev(k):
        return (dp, y * RING + (z + k) % RING)

    def xdev(k):
        return (((x + k) % RING) * 2 + c, ex)

    a_dev = (ydev, zdev)
    b_dev = (zdev, ydev)
    partner = (x * 2 + 1 - c, ex)

    def rcopy(src, dst, ss, rs, dev):
        return pltpu.make_async_remote_copy(
            src_ref=src, dst_ref=dst, send_sem=ss, recv_sem=rs, device_id=dev, device_id_type=MESH
        )

    def load_w(j):
        return pltpu.make_async_copy(w_hbm.at[j], W, w_sem)

    load_w(0).start()

    barrier = pltpu.get_barrier_semaphore()
    peers = [ydev(k) for k in (1, 2, 3)] + [zdev(k) for k in (1, 2, 3)] + [xdev(1), xdev(3), partner]
    for dev in peers:
        pl.semaphore_signal(barrier, inc=1, device_id=dev, device_id_type=MESH)

    for p in (0, 1):
        RT[p, a_me[p]] = rt[...]
    AG[1, z] = ug[...]
    low = lh[...].astype(F32)
    scale = lax.rsqrt(jnp.mean(low * low, axis=1, keepdims=True) + NORM_EPS)
    AG[0, y] = (low * scale).astype(BF16)

    pl.semaphore_wait(barrier, len(peers))

    HALF = T // 2

    def rows(h):
        return pl.ds(h * HALF, HALF)

    def rt_copy(p, k):
        me = a_me[p]
        return rcopy(RT.at[p, me], RT.at[p, me], rt_s.at[p, k], rt_r.at[p, k], a_dev[p](k))

    def ag_copy(p, d, h):
        me = a_me[p]
        blk = AG.at[p, me, rows(h)]
        return rcopy(blk, blk, ag_s.at[p, d, h], ag_r.at[p, d, h], a_dev[p](1 if d == 0 else 3))

    def agf_copy(p, d):
        frm = (a_me[p] + (3 if d == 0 else 1)) % RING
        blk = AG.at[p, frm, rows(d)]
        return rcopy(blk, blk, agf_s.at[p, d], agf_r.at[p, d], a_dev[p](1 if d == 0 else 3))

    for p in (1, 0):
        for k in (1, 2, 3):
            rt_copy(p, k).start()
    for p in (1, 0):
        ag_copy(p, 0, 0).start()
        ag_copy(p, 1, 1).start()
    for p in (1, 0):
        ag_copy(p, 0, 1).start()
        ag_copy(p, 1, 0).start()

    row = lax.broadcasted_iota(jnp.int32, (T, T), 0)

    def codes_of(p, j):
        b, s = row >> 5, row & 31
        if p == 0:
            return 64 * (4 * y + b) + 32 * j + s
        return 64 * (4 * b + z) + 32 * j + s

    def onehot(p, j, a):
        val = codes_of(p, j)
        hot = jnp.zeros((T, T), F32)
        share = jnp.zeros((T, T), F32)
        for k in range(TOPK):
            m = RT[p, a, k : k + 1, :] == val
            hot = jnp.where(m, 1.0, hot)
            gate = RT[p, a, 8 + k : 9 + k, :].astype(F32) * (1.0 / GATE_DENOM)
            share = jnp.where(m, gate, share)
        return hot, share

    def gather(p, j, a):
        hot, share = onehot(p, j, a)
        hot = hot.astype(BF16)
        for n in range(4):
            cols = pl.ds(n * 512, 512)
            picked = dot_nn(hot, AG[p, a, :, cols])
            if p == 1:
                picked = picked * jnp.sum(share, axis=1, keepdims=True)
            SD[p, j, a, :, cols] = picked.astype(BF16)

    def r_rows(p, a):
        block = a * RING + z if p == 0 else y * RING + a
        return pl.ds(pl.multiple_of(block * S, S), S)

    def r_rows_of(p, a, b):
        block = a * RING + b if p == 0 else b * RING + a
        return pl.ds(pl.multiple_of(block * S, S), S)

    def slots(b):
        return pl.ds(pl.multiple_of(b * S, S), S)

    def s2_send(p, j, a):
        for k in (1, 2, 3):
            b = (b_me[p] + k) % RING
            rcopy(
                SD.at[p, j, a, slots(b)], R.at[p, j, r_rows(p, a)],
                s2_s.at[p, j, k], s2_r.at[p, j, k], b_dev[p](k),
            ).start()
        pltpu.make_async_copy(
            SD.at[p, j, a, slots(b_me[p])], R.at[p, j, r_rows(p, a)], loc.at[p, j]
        ).start()

    def s2_whole(p, j, k):
        return rcopy(SD.at[p, j, 0], R.at[p, j, pl.ds(0, T)], s2_s.at[p, j, k], s2_r.at[p, j, k], b_dev[p](k))

    def loc_whole(p, j):
        return pltpu.make_async_copy(SD.at[p, j, 0], R.at[p, j, pl.ds(0, T)], loc.at[p, j])

    for p in (1, 0):
        gather(p, 0, a_me[p])
        s2_send(p, 0, a_me[p])
    for p in (1, 0):
        ag_copy(p, 0, 0).wait_recv()
        agf_copy(p, 0).start()
        ag_copy(p, 1, 1).wait_recv()
        agf_copy(p, 1).start()
    for p in (1, 0):
        for k in (1, 2, 3):
            rt_copy(p, k).wait_recv()
    for p in (1, 0):
        ag_copy(p, 0, 1).wait_recv()
        gather(p, 0, (a_me[p] + 3) % RING)
        s2_send(p, 0, (a_me[p] + 3) % RING)
        ag_copy(p, 1, 0).wait_recv()
        gather(p, 0, (a_me[p] + 1) % RING)
        s2_send(p, 0, (a_me[p] + 1) % RING)
    for p in (1, 0):
        agf_copy(p, 0).wait_recv()
        agf_copy(p, 1).wait_recv()
        gather(p, 0, (a_me[p] + 2) % RING)
        s2_send(p, 0, (a_me[p] + 2) % RING)

    def gather_later(a, carry):
        for p in (1, 0):
            gather(p, 1, a)
        return carry

    lax.fori_loop(0, RING, gather_later, 0)
    for p in (1, 0):
        for k in (1, 2, 3):
            rt_copy(p, k).wait_send()
        for d in (0, 1):
            for h in (0, 1):
                ag_copy(p, d, h).wait_send()
            agf_copy(p, d).wait_send()

    def s2_sent(j):
        for p in (0, 1):
            for k in (1, 2, 3):
                s2_whole(p, j, k).wait_send()
            loc_whole(p, j).wait()
        for p in (0, 1):
            for k in (1, 2, 3):
                pl.semaphore_signal(credit.at[j], inc=1, device_id=b_dev[p](k), device_id_type=MESH)

    s2_sent(0)

    def send_later(a, carry):
        for p in (1, 0):
            s2_send(p, 1, a)
        return carry

    lax.fori_loop(0, RING, send_later, 0)

    def px_copy(p, j, b):
        src = R.at[p, j, :, pl.ds(pl.multiple_of(b * 512 + (1 - c) * SHARE, SHARE), SHARE)]
        return rcopy(src, PX.at[p, :, pl.ds(b * SHARE, SHARE)], px_s.at[p], px_r.at[p], partner)

    def px_whole(p):
        half = R.at[p, 0, :, pl.ds(0, 4 * SHARE)]
        return rcopy(half, PX.at[p], px_s.at[p], px_r.at[p], partner)

    def pg_copy(cols):
        return rcopy(G.at[:, cols], PG.at[:, cols], pg_s, pg_r, partner)

    pg_whole = rcopy(G, PG, pg_s, pg_r, partner)

    def hidden_part(j):
        for p in (0, 1):
            for k in (1, 2, 3):
                s2_whole(p, j, k).wait_recv()
        if j == 1:
            pl.semaphore_wait(pcredit, 1)
        for p in (0, 1):
            for b in range(RING):
                px_copy(p, j, b).start()
        load_w(j).wait()

        def tile(n, carry):
            at = [pl.ds(pl.multiple_of(i * H + n * 256, 256), 256) for i in range(3)]
            gate = dot_nn(R[0, j], W[:, at[0]])
            up = dot_nn(R[0, j], W[:, at[1]])
            grad = dot_nn(R[1, j], W[:, at[2]])
            sig = jax.nn.sigmoid(gate)
            act = gate * sig
            G[:, at[2]] = (act * up).astype(BF16)
            G[:, at[0]] = (grad * up * sig * (1.0 + gate * (1.0 - sig))).astype(BF16)
            G[:, at[1]] = (grad * act).astype(BF16)
            for i in range(3):
                pg_copy(at[i]).start()
            return carry

        lax.fori_loop(0, 3, tile, 0)

    def outputs_part(j, out, route):
        def tile(n, carry):
            at = pl.ds(pl.multiple_of(n * 256, 256), 256)
            out[:, at] = dot_nt(G[:, 2 * H :], W[at, 2 * H :]).astype(BF16)
            route[:, at] = dot_nt(G[:, : 2 * H], W[at, : 2 * H]).astype(BF16)
            return carry

        lax.fori_loop(0, D // 256, tile, 0)

    def weight_block(j, b, dst):
        mine = pl.ds(pl.multiple_of(b * 512 + c * SHARE, SHARE), SHARE)
        theirs = pl.ds(pl.multiple_of(b * SHARE, SHARE), SHARE)

        def tile(p, first, count):
            def body(n, carry):
                at = pl.ds(pl.multiple_of(first + n * 256, 256), 256)
                acc = dot_tn(R[p, j, :, mine], G[:, at])
                acc = acc + dot_tn(PX[p, :, theirs], PG[:, at])
                dst[:, at] = acc.astype(BF16)
                return carry

            lax.fori_loop(0, count, body, 0)

        tile(0, 0, 6)
        tile(1, 2 * H, 3)

    AH = pl.ds(0, SHARE // 2)
    BH = pl.ds(SHARE // 2, SHARE // 2)

    def x_copy(j, own, d, i):
        to = xdev(1 if d == 0 else 3)
        near = own((x + (1 if d == 0 else 3)) % RING)
        far = own((x + 2) % RING)
        fin = o_left if d == 0 else o_right
        early, late = (AH, BH) if d == 0 else (BH, AH)
        if i == 0:
            src, dst = far.at[early], TMP.at[j, d]
        elif i == 1:
            src, dst = near.at[late], fin.at[j, late]
        else:
            src, dst = near.at[early], fin.at[j, early]
        return rcopy(src, dst, x_s.at[j, d, i], x_r.at[j, d, i], to)

    def own_copy(j, own):
        return pltpu.make_async_copy(own(x), o_own.at[j], w_sem)

    def weight_part(j, own):
        for p in (0, 1):
            px_whole(p).wait_recv()
        pg_whole.wait_recv()
        weight_block(j, (x + 2) % RING, own((x + 2) % RING))
        x_copy(j, own, 0, 0).start()
        x_copy(j, own, 1, 0).start()
        weight_block(j, (x + 1) % RING, own((x + 1) % RING))
        x_copy(j, own, 0, 1).start()
        weight_block(j, (x + 3) % RING, own((x + 3) % RING))
        x_copy(j, own, 1, 1).start()
        weight_block(j, x, own(x))
        if j == 0:
            pl.semaphore_signal(pcredit, inc=1, device_id=partner, device_id_type=MESH)

    def partner_sent():
        for p in (0, 1):
            px_whole(p).wait_send()
        pg_whole.wait_send()

    def x_add(j, own):
        for d in (0, 1):
            early = AH if d == 0 else BH
            near = own((x + (1 if d == 0 else 3)) % RING)
            x_copy(j, own, d, 0).wait_recv()
            near[early, :] = (near[early, :].astype(F32) + TMP[j, d].astype(F32)).astype(BF16)
            x_copy(j, own, d, 2).start()

    def x_done(j, own):
        for d in (0, 1):
            for i in (1, 2):
                x_copy(j, own, d, i).wait_recv()
            for i in range(3):
                x_copy(j, own, d, i).wait_send()

    def own0(b):
        return OWN.at[b]

    def own1(b):
        return W.at[pl.ds(pl.multiple_of(b * SHARE, SHARE), SHARE)]

    def back(j, bufs):
        pl.semaphore_wait(credit.at[j], 6)
        for p in (0, 1):
            for k in (1, 2, 3):
                b = (b_me[p] + k) % RING
                for a in range(RING):
                    rcopy(
                        bufs[p].at[r_rows_of(p, a, b)], SD.at[p, j, a, slots(b_me[p])],
                        rb_s.at[p, j, k], rb_r.at[p, j, k], b_dev[p](k),
                    ).start()
            for a in range(RING):
                pltpu.make_async_copy(
                    bufs[p].at[r_rows(p, a)], SD.at[p, j, a, slots(b_me[p])], loc.at[p, j]
                ).start()

    def back_whole(p, j, k, bufs):
        return rcopy(
            bufs[p].at[pl.ds(0, T)], SD.at[p, j, 0], rb_s.at[p, j, k], rb_r.at[p, j, k], b_dev[p](k)
        )

    bufs0 = (R.at[0, 0], R.at[1, 0])
    bufs1 = (O1.at[0], O1.at[1])

    hidden_part(0)
    weight_part(0, own0)
    partner_sent()
    outputs_part(0, bufs0[0], bufs0[1])
    load_w(1).start()
    back(0, bufs0)
    s2_sent(1)
    hidden_part(1)
    x_add(0, own0)
    outputs_part(1, bufs1[0], bufs1[1])
    back(1, bufs1)
    weight_part(1, own1)
    partner_sent()
    own_copy(0, own0).start()
    own_copy(0, own0).wait()
    own_copy(1, own1).start()

    def fn_copy(p, d, i):
        to = a_dev[p](1 if d == 0 else 3)
        near = (a_me[p] + (1 if d == 0 else 3)) % RING
        far = (a_me[p] + 2) % RING
        fin = FL if d == 0 else FR
        early, late = rows(d), rows(1 - d)
        if i == 0:
            src, dst = AG.at[p, far, early], FT.at[p, d]
        elif i == 1:
            src, dst = AG.at[p, near, late], fin.at[p, late]
        else:
            src, dst = AG.at[p, near, early], fin.at[p, early]
        return rcopy(src, dst, fn_s.at[p, d, i], fn_r.at[p, d, i], to)

    def combine(p, a):
        parts = []
        for j in (0, 1):
            hot, share = onehot(p, j, a)
            if p == 0:
                top = share.astype(BF16)
                parts.append((j, top))
                parts.append((j, (share - top.astype(F32)).astype(BF16)))
            else:
                parts.append((j, hot.astype(BF16)))
        for n in range(4):
            cols = pl.ds(n * 512, 512)
            total = jnp.zeros((T, 512), F32)
            for j, weights in parts:
                total = total + dot_tn(weights, SD[p, j, a, :, cols])
            AG[p, a, :, cols] = total.astype(BF16)

    for p in (0, 1):
        for j, bufs in ((0, bufs0), (1, bufs1)):
            for k in (1, 2, 3):
                back_whole(p, j, k, bufs).wait_recv()
            loc_whole(p, j).wait()
        combine(p, (a_me[p] + 2) % RING)
        fn_copy(p, 0, 0).start()
        fn_copy(p, 1, 0).start()
        combine(p, (a_me[p] + 1) % RING)
        fn_copy(p, 0, 1).start()
        combine(p, (a_me[p] + 3) % RING)
        fn_copy(p, 1, 1).start()
    for p in (0, 1):
        combine(p, a_me[p])
    for p in (0, 1):
        for d in (0, 1):
            near = (a_me[p] + (1 if d == 0 else 3)) % RING
            early = rows(d)
            fn_copy(p, d, 0).wait_recv()
            AG[p, near, early, :] = (
                AG[p, near, early, :].astype(F32) + FT[p, d].astype(F32)
            ).astype(BF16)
            fn_copy(p, d, 2).start()

    x_add(1, own1)

    for p in (0, 1):
        for d in (0, 1):
            for i in (1, 2):
                fn_copy(p, d, i).wait_recv()
    mixture = AG[0, y].astype(F32) + FL[0].astype(F32) + FR[0].astype(F32)
    o_up[...] = (uh[...].astype(F32) - mixture).astype(BF16)
    grad_normed = AG[1, z].astype(F32) + FL[1].astype(F32) + FR[1].astype(F32)
    low = lh[...].astype(F32)
    scale = lax.rsqrt(jnp.mean(low * low, axis=1, keepdims=True) + NORM_EPS)
    inner = jnp.mean(low * grad_normed, axis=1, keepdims=True)
    o_lo[...] = (
        lg[...].astype(F32) + scale * grad_normed - low * (scale * scale * scale) * inner
    ).astype(BF16)

    for p in (0, 1):
        for d in (0, 1):
            for i in range(3):
                fn_copy(p, d, i).wait_send()
        for j, bufs in ((0, bufs0), (1, bufs1)):
            for k in (1, 2, 3):
                back_whole(p, j, k, bufs).wait_send()
    own_copy(1, own1).wait()
    x_done(0, own0)
    x_done(1, own1)


def run(upper_half, lower_half, upper_grad, lower_grad, routes, expert_weight):
    vm = pl.BlockSpec(memory_space=pltpu.VMEM)
    hbm = pl.BlockSpec(memory_space=pl.ANY)
    dma = pltpu.SemaphoreType.DMA
    half = jax.ShapeDtypeStruct((2, SHARE, F), BF16)
    rows = jax.ShapeDtypeStruct((T, D), BF16)
    return pl.pallas_call(
        kernel,
        out_shape=(rows, rows, half, half, half),
        in_specs=[vm, vm, vm, vm, vm, hbm],
        out_specs=(vm, vm, hbm, hbm, hbm),
        scratch_shapes=[
            pltpu.VMEM((2, RING, T, D), BF16),
            pltpu.VMEM((2, RING, 16, T), jnp.int32),
            pltpu.VMEM((2, 2, RING, T, D), BF16),
            pltpu.VMEM((2, 2, M, D), BF16),
            pltpu.VMEM((2, M, D), BF16),
            pltpu.VMEM((D, F), BF16),
            pltpu.VMEM((M, F), BF16),
            pltpu.VMEM((2, M, 4 * SHARE), BF16),
            pltpu.VMEM((M, F), BF16),
            pltpu.VMEM((RING, SHARE, F), BF16),
            pltpu.VMEM((2, 2, SHARE // 2, F), BF16),
            pltpu.VMEM((2, T, D), BF16),
            pltpu.VMEM((2, T, D), BF16),
            pltpu.VMEM((2, 2, T // 2, D), BF16),
            dma((2, 2, 2)), dma((2, 2, 2)),
            dma((2, 2)), dma((2, 2)),
            dma((2, 4)), dma((2, 4)),
            dma((2, 2, 4)), dma((2, 2, 4)),
            dma((2, 2, 4)), dma((2, 2, 4)),
            dma((2,)), dma((2,)),
            dma, dma,
            dma((2, 2, 3)), dma((2, 2, 3)),
            dma((2, 2, 3)), dma((2, 2, 3)),
            dma((2, 2)),
            dma,
            pltpu.SemaphoreType.REGULAR((2,)),
            pltpu.SemaphoreType.REGULAR,
        ],
        compiler_params=pltpu.CompilerParams(
            collective_id=0, has_side_effects=True, vmem_limit_bytes=61 * 1024 * 1024
        ),
        cost_estimate=pl.CostEstimate(
            flops=29_000_000_000, bytes_accessed=30_000_000, transcendentals=800_000
        ),
    )(upper_half, lower_half, upper_grad, lower_grad, routes, expert_weight)


def shards(
    upper_half, lower_half, upper_grad, lower_grad, expert_ids, gate_weights, route_slots, expert_weight
):
    code = jnp.where(route_slots < CAP, expert_ids * S + route_slots, -1)
    pad = ((0, 0), (0, 8 - TOPK))
    routes = jnp.concatenate(
        [jnp.pad(code, pad, constant_values=-1), jnp.pad(gate_weights, pad)], axis=1
    ).T
    up, lo, own, left, right = run(
        upper_half, lower_half, upper_grad, lower_grad, routes, expert_weight
    )
    weight_grad = own.astype(F32) + left.astype(F32) + right.astype(F32)
    return up, lo, weight_grad


def solution(mesh):
    tok = P(("dp", "expert"), None)
    return jax.shard_map(
        shards,
        mesh=mesh,
        in_specs=(tok,) * 7 + (P("expert", None, None),),
        out_specs=(tok, tok, P("expert", "dp", None)),
        check_vma=False,
    )
```

time: 422 us -> 165 us (0.39); the launches traced: 414 us -> 164 us
  Pallas kernels: 0 us -> 154 us
  local copies, waits for them, and re-layouts: 132 us -> 1.59 us
  waiting for transfers between devices: 128 us -> 0 us
  matrix products: 54.1 us -> 0 us
  other arithmetic: 54.8 us -> 8.11 us
  starting transfers between devices: 30.9 us -> 0 us
  between operations: 14.6 us -> 0.66 us
    pallas_call x0 -> x1, Pallas kernels: none -> 154 us  [run(): pl.pallas_call(kernel, out_shape=(rows, rows, half, half, half), in_specs...]
    all_to_all x4 -> x0, waiting for transfers between devices: 128 us -> none  [the longest x1 44.5 us: shards(): lax.all_to_all(normed_send, 'expert', split_axis=0, concat_axis=0, tiled=...]
    dot_general x8 -> x0, matrix products: 54.1 us -> none  [the longest x1 15.3 us: expert_forward(): jnp.einsum('sjcd,jdf->sjcf', normed_rows, expert_weight[:, :, :2 * hidden...]
    reshape x8 -> x0, local copies, waits for them, and re-layouts: 41.6 us -> none  [the longest x2 13.3 us: shards(): scatter_rows(repeated, route_index, slots_total).reshape(send_shape)]
    all_to_all x4 -> x0, starting transfers between devices: 30.9 us -> none  [the longest x1 10.5 us: shards(): lax.all_to_all(normed_send, 'expert', split_axis=0, concat_axis=0, tiled=...]
    gather x4 -> x0, local copies, waits for them, and re-layouts: 23.7 us -> none  [the longest x2 11.9 us: shards(): jnp.take(output_flat, flat_index, axis=0, mode='fill', fill_value=0)]
    concatenate x2 -> x0, other arithmetic: 23 us -> none  [weight_term(): return jnp.concatenate([upper_block, lower_block], axis=1)]
    all_to_all x4 -> x0, local copies, waits for them, and re-layouts: 21.9 us -> none  [the longest x1 6.05 us: shards(): lax.all_to_all(output, 'expert', split_axis=0, concat_axis=0, tiled=True)]
  transfers between devices with their start and end apart: 6 -> 0, of which waited for: 4 -> 0; matrix products, arithmetic and copies ran while one was open for 34% -> 0% of each run, Pallas kernels for 0% -> 0%
where the time goes in v1:
time: 165 us; the launch traced here: 164 us
  Pallas kernels  154 us (93%)
  other arithmetic  8.11 us (5%)
    pallas_call x1, Pallas kernels, run(): pl.pallas_call(kernel, out_shape=(rows, rows, half, half, half), in_specs...  154 us
    add x1, other arithmetic, shards(): weight_grad = own.astype(F32) + left.astype(F32) + right.astype(F32)  6.12 us

profile of v1, /device:TPU:0, one launch (start us, length us, event | category | flops | bytes accessed | tf_op | source)
XLA Modules:
  0.0 164.2 jit_solution(10933467569430185995)
XLA Ops:
  0.6 0.7 add_select_fusion
  1.3 1.3 fusion.rt
  2.6 153.8 %shard_map.103 = (bf16[128,2048]{1,0:T(8,128)(2,1)}, bf16[128,2048]{1,0:T(8,128)(2,1)}, bf16[2,256,2304]{2,1,0:T(8,128)(2,1)}, bf16[2,256,2304]{2,1,0:T(8,128)(2,1)}, bf16[2,256,2304]{2,1,0:T(8,128)(2,1)}) custom-call(bf16[128,2048]{1,0:T(8,128)(2,1)} %uh.1, bf16[128,2048]{1,0:T(8,128)(2,1)} %lh.1, bf16[128,2048]{1,0:T(8,128)(2,1)} %ug.1, ...), custom_call_target="tpu_custom_call" | custom-call | flops 28999999488 | bytes 30000000 | tf_op jit(solution)/shard_map/pallas_call | solution.py:489
  156.5 0.0 copy-start.1
  156.5 0.0 copy-start
  156.5 6.1 %convert_add_fusion = f32[2,256,2304]{2,1,0:T(8,128)} fusion(bf16[2,256,2304]{2,1,0:T(8,128)(2,1)} %get-tuple-element.12, bf16[2,256,2304]{2,1,0:T(8,128)(2,1)} %get-tuple-element.11, bf16[2,256,2304]{2,1,0:T(8,128)(2,1)} %get-tuple-element.10), kind=kLoop, calls=%fused_computation | loop fusion | flops 5898240 | bytes 11796480 | tf_op jit(solution)/shard_map/add | solution.py:543
  162.6 0.0 copy-done.1
  162.6 0.8 copy.13
  163.4 0.0 copy-done
  163.4 0.8 copy.14
Async XLA Ops:
  156.5 6.1 %copy-start.1 = (bf16[128,2048]{1,0:T(8,128)(2,1)S(1)}, bf16[128,2048]{1,0:T(8,128)(2,1)}, u32[]{:S(2)}) copy-start(bf16[128,2048]{1,0:T(8,128)(2,1)} %get-tuple-element.16) | copy-start | bytes 1572868
  156.5 6.9 %copy-start = (bf16[128,2048]{1,0:T(8,128)(2,1)S(1)}, bf16[128,2048]{1,0:T(8,128)(2,1)}, u32[]{:S(2)}) copy-start(bf16[128,2048]{1,0:T(8,128)(2,1)} %get-tuple-element.17) | copy-start | bytes 1572868

commit v2 on v1

--- a/solution.py
+++ b/solution.py
@@ -38,11 +38,11 @@
 
 
 def kernel(
-    uh, lh, ug, lg, rt, w_hbm,
+    uh_in, lh_in, ug_in, lg_in, ids_in, gates_in, slots_in, w_hbm,
     o_up, o_lo, o_own, o_left, o_right,
-    AG, RT, SD, R, O1, W, G, PX, PG, OWN, TMP, FL, FR, FT,
+    uh, lh, lg, ids, gates, slots_of, AG, RT, SD, R, O, W, G, PX, PG, OWN, TMP, FL, FR, FT,
     ag_s, ag_r, agf_s, agf_r, rt_s, rt_r, s2_s, s2_r, rb_s, rb_r,
-    px_s, px_r, pg_s, pg_r, x_s, x_r, fn_s, fn_r, loc, w_sem, credit, pcredit,
+    px_s, px_r, pg_s, pg_r, x_s, x_r, fn_s, fn_r, loc, loc_b, w_sem, in_sem, credit, pcredit,
 ):
     dp = lax.axis_index("dp")
     ex = lax.axis_index("expert")
@@ -72,19 +72,29 @@
     def load_w(j):
         return pltpu.make_async_copy(w_hbm.at[j], W, w_sem)
 
-    load_w(0).start()
-
     barrier = pltpu.get_barrier_semaphore()
     peers = [ydev(k) for k in (1, 2, 3)] + [zdev(k) for k in (1, 2, 3)] + [xdev(1), xdev(3), partner]
     for dev in peers:
         pl.semaphore_signal(barrier, inc=1, device_id=dev, device_id_type=MESH)
 
+    pairs = (
+        (lh_in, lh), (ug_in, AG.at[1, z]), (ids_in, ids), (gates_in, gates), (slots_in, slots_of),
+        (uh_in, uh), (lg_in, lg),
+    )
+    loads = [pltpu.make_async_copy(src, dst, in_sem.at[i]) for i, (src, dst) in enumerate(pairs)]
+    for load in loads:
+        load.start()
+    load_w(0).start()
+    for i in (2, 3, 4):
+        loads[i].wait()
     for p in (0, 1):
-        RT[p, a_me[p]] = rt[...]
-    AG[1, z] = ug[...]
+        RT[p, a_me[p], 0:TOPK, :] = jnp.where(slots_of[...] < CAP, ids[...] * S + slots_of[...], -1)
+        RT[p, a_me[p], 8 : 8 + TOPK, :] = gates[...]
+    loads[0].wait()
     low = lh[...].astype(F32)
     scale = lax.rsqrt(jnp.mean(low * low, axis=1, keepdims=True) + NORM_EPS)
     AG[0, y] = (low * scale).astype(BF16)
+    loads[1].wait()
 
     pl.semaphore_wait(barrier, len(peers))
 
@@ -313,23 +323,21 @@
             src, dst = near.at[early], fin.at[j, early]
         return rcopy(src, dst, x_s.at[j, d, i], x_r.at[j, d, i], to)
 
-    def own_copy(j, own):
-        return pltpu.make_async_copy(own(x), o_own.at[j], w_sem)
-
-    def weight_part(j, own):
+    def weight_far(j, own):
         for p in (0, 1):
             px_whole(p).wait_recv()
         pg_whole.wait_recv()
         weight_block(j, (x + 2) % RING, own((x + 2) % RING))
         x_copy(j, own, 0, 0).start()
         x_copy(j, own, 1, 0).start()
-        weight_block(j, (x + 1) % RING, own((x + 1) % RING))
-        x_copy(j, own, 0, 1).start()
-        weight_block(j, (x + 3) % RING, own((x + 3) % RING))
-        x_copy(j, own, 1, 1).start()
+
+    def weight_near(j, own, d):
+        b = (x + (1 if d == 0 else 3)) % RING
+        weight_block(j, b, own(b))
+        x_copy(j, own, d, 1).start()
+
+    def weight_own(j, own):
         weight_block(j, x, own(x))
-        if j == 0:
-            pl.semaphore_signal(pcredit, inc=1, device_id=partner, device_id_type=MESH)
 
     def partner_sent():
         for p in (0, 1):
@@ -357,45 +365,65 @@
     def own1(b):
         return W.at[pl.ds(pl.multiple_of(b * SHARE, SHARE), SHARE)]
 
-    def back(j, bufs):
-        pl.semaphore_wait(credit.at[j], 6)
-        for p in (0, 1):
+    OFFS = (2, 1, 3, 0)
+
+    def back(j, i):
+        for p in (0, 1):
+            a = (a_me[p] + OFFS[i]) % RING
             for k in (1, 2, 3):
                 b = (b_me[p] + k) % RING
-                for a in range(RING):
-                    rcopy(
-                        bufs[p].at[r_rows_of(p, a, b)], SD.at[p, j, a, slots(b_me[p])],
-                        rb_s.at[p, j, k], rb_r.at[p, j, k], b_dev[p](k),
-                    ).start()
-            for a in range(RING):
-                pltpu.make_async_copy(
-                    bufs[p].at[r_rows(p, a)], SD.at[p, j, a, slots(b_me[p])], loc.at[p, j]
+                rcopy(
+                    O.at[p, j, r_rows_of(p, a, b)], SD.at[p, j, a, slots(b_me[p])],
+                    rb_s.at[p, j, k], rb_r.at[p, j, i], b_dev[p](k),
                 ).start()
-
-    def back_whole(p, j, k, bufs):
-        return rcopy(
-            bufs[p].at[pl.ds(0, T)], SD.at[p, j, 0], rb_s.at[p, j, k], rb_r.at[p, j, k], b_dev[p](k)
-        )
-
-    bufs0 = (R.at[0, 0], R.at[1, 0])
-    bufs1 = (O1.at[0], O1.at[1])
+            pltpu.make_async_copy(
+                O.at[p, j, r_rows(p, a)], SD.at[p, j, a, slots(b_me[p])], loc_b.at[p, j, i]
+            ).start()
+
+    def back_arrived(p, j, i):
+        rcopy(
+            O.at[p, j, pl.ds(0, 3 * S)], SD.at[p, j, 0, pl.ds(0, 3 * S)],
+            rb_s.at[p, j, 1], rb_r.at[p, j, i], b_dev[p](1),
+        ).wait_recv()
+        pltpu.make_async_copy(
+            O.at[p, j, pl.ds(0, S)], SD.at[p, j, 0, pl.ds(0, S)], loc_b.at[p, j, i]
+        ).wait()
+
+    def back_sent(p, j, k):
+        rcopy(
+            O.at[p, j, pl.ds(0, T)], SD.at[p, j, 0], rb_s.at[p, j, k], rb_r.at[p, j, 0], b_dev[p](k)
+        ).wait_send()
 
     hidden_part(0)
-    weight_part(0, own0)
+    weight_far(0, own0)
+    outputs_part(0, O.at[0, 0], O.at[1, 0])
+    load_w(1).start()
+    pl.semaphore_wait(credit.at[0], 6)
+    for i in range(RING):
+        back(0, i)
+    weight_near(0, own0, 0)
+    weight_near(0, own0, 1)
+    weight_own(0, own0)
+    pl.semaphore_signal(pcredit, inc=1, device_id=partner, device_id_type=MESH)
     partner_sent()
-    outputs_part(0, bufs0[0], bufs0[1])
-    load_w(1).start()
-    back(0, bufs0)
     s2_sent(1)
     hidden_part(1)
     x_add(0, own0)
-    outputs_part(1, bufs1[0], bufs1[1])
-    back(1, bufs1)
-    weight_part(1, own1)
+    outputs_part(1, O.at[0, 1], O.at[1, 1])
+    pl.semaphore_wait(credit.at[1], 6)
+    back(1, 0)
+    weight_far(1, own1)
+    back(1, 1)
+    weight_near(1, own1, 0)
+    back(1, 2)
+    weight_near(1, own1, 1)
+    back(1, 3)
+    weight_own(1, own1)
     partner_sent()
-    own_copy(0, own0).start()
-    own_copy(0, own0).wait()
-    own_copy(1, own1).start()
+    own_copies = [pltpu.make_async_copy(own(x), o_own.at[j], w_sem) for j, own in enumerate((own0, own1))]
+    own_copies[0].start()
+    own_copies[0].wait()
+    own_copies[1].start()
 
     def fn_copy(p, d, i):
         to = a_dev[p](1 if d == 0 else 3)
@@ -428,36 +456,34 @@
                 total = total + dot_tn(weights, SD[p, j, a, :, cols])
             AG[p, a, :, cols] = total.astype(BF16)
 
-    for p in (0, 1):
-        for j, bufs in ((0, bufs0), (1, bufs1)):
-            for k in (1, 2, 3):
-                back_whole(p, j, k, bufs).wait_recv()
-            loc_whole(p, j).wait()
-        combine(p, (a_me[p] + 2) % RING)
-        fn_copy(p, 0, 0).start()
-        fn_copy(p, 1, 0).start()
-        combine(p, (a_me[p] + 1) % RING)
-        fn_copy(p, 0, 1).start()
-        combine(p, (a_me[p] + 3) % RING)
-        fn_copy(p, 1, 1).start()
-    for p in (0, 1):
-        combine(p, a_me[p])
-    for p in (0, 1):
-        for d in (0, 1):
-            near = (a_me[p] + (1 if d == 0 else 3)) % RING
-            early = rows(d)
-            fn_copy(p, d, 0).wait_recv()
-            AG[p, near, early, :] = (
-                AG[p, near, early, :].astype(F32) + FT[p, d].astype(F32)
-            ).astype(BF16)
-            fn_copy(p, d, 2).start()
-
-    x_add(1, own1)
+    for i in range(RING):
+        if i == 3:
+            for p in (0, 1):
+                for d in (0, 1):
+                    near = (a_me[p] + (1 if d == 0 else 3)) % RING
+                    early = rows(d)
+                    fn_copy(p, d, 0).wait_recv()
+                    AG[p, near, early, :] = (
+                        AG[p, near, early, :].astype(F32) + FT[p, d].astype(F32)
+                    ).astype(BF16)
+                    fn_copy(p, d, 2).start()
+            x_add(1, own1)
+        for p in (0, 1):
+            for j in (0, 1):
+                back_arrived(p, j, i)
+            combine(p, (a_me[p] + OFFS[i]) % RING)
+            if i == 0:
+                fn_copy(p, 0, 0).start()
+                fn_copy(p, 1, 0).start()
+            elif i < 3:
+                fn_copy(p, i - 1, 1).start()
 
     for p in (0, 1):
         for d in (0, 1):
             for i in (1, 2):
                 fn_copy(p, d, i).wait_recv()
+    loads[5].wait()
+    loads[6].wait()
     mixture = AG[0, y].astype(F32) + FL[0].astype(F32) + FR[0].astype(F32)
     o_up[...] = (uh[...].astype(F32) - mixture).astype(BF16)
     grad_normed = AG[1, z].astype(F32) + FL[1].astype(F32) + FR[1].astype(F32)
@@ -472,15 +498,15 @@
         for d in (0, 1):
             for i in range(3):
                 fn_copy(p, d, i).wait_send()
-        for j, bufs in ((0, bufs0), (1, bufs1)):
+        for j in (0, 1):
             for k in (1, 2, 3):
-                back_whole(p, j, k, bufs).wait_send()
-    own_copy(1, own1).wait()
+                back_sent(p, j, k)
+    own_copies[1].wait()
     x_done(0, own0)
     x_done(1, own1)
 
 
-def run(upper_half, lower_half, upper_grad, lower_grad, routes, expert_weight):
+def run(*arrays):
     vm = pl.BlockSpec(memory_space=pltpu.VMEM)
     hbm = pl.BlockSpec(memory_space=pl.ANY)
     dma = pltpu.SemaphoreType.DMA
@@ -489,14 +515,20 @@
     return pl.pallas_call(
         kernel,
         out_shape=(rows, rows, half, half, half),
-        in_specs=[vm, vm, vm, vm, vm, hbm],
+        in_specs=[hbm] * 8,
         out_specs=(vm, vm, hbm, hbm, hbm),
         scratch_shapes=[
+            pltpu.VMEM((T, D), BF16),
+            pltpu.VMEM((T, D), BF16),
+            pltpu.VMEM((T, D), BF16),
+            pltpu.VMEM((TOPK, T), jnp.int32),
+            pltpu.VMEM((TOPK, T), jnp.int32),
+            pltpu.VMEM((TOPK, T), jnp.int32),
             pltpu.VMEM((2, RING, T, D), BF16),
             pltpu.VMEM((2, RING, 16, T), jnp.int32),
             pltpu.VMEM((2, 2, RING, T, D), BF16),
             pltpu.VMEM((2, 2, M, D), BF16),
-            pltpu.VMEM((2, M, D), BF16),
+            pltpu.VMEM((2, 2, M, D), BF16),
             pltpu.VMEM((D, F), BF16),
             pltpu.VMEM((M, F), BF16),
             pltpu.VMEM((2, M, 4 * SHARE), BF16),
@@ -516,29 +548,27 @@
             dma((2, 2, 3)), dma((2, 2, 3)),
             dma((2, 2, 3)), dma((2, 2, 3)),
             dma((2, 2)),
+            dma((2, 2, 4)),
             dma,
+            dma((7,)),
             pltpu.SemaphoreType.REGULAR((2,)),
             pltpu.SemaphoreType.REGULAR,
         ],
         compiler_params=pltpu.CompilerParams(
-            collective_id=0, has_side_effects=True, vmem_limit_bytes=61 * 1024 * 1024
+            collective_id=0, has_side_effects=True, vmem_limit_bytes=63 * 1024 * 1024
         ),
         cost_estimate=pl.CostEstimate(
             flops=29_000_000_000, bytes_accessed=30_000_000, transcendentals=800_000
         ),
-    )(upper_half, lower_half, upper_grad, lower_grad, routes, expert_weight)
+    )(*arrays)
 
 
 def shards(
     upper_half, lower_half, upper_grad, lower_grad, expert_ids, gate_weights, route_slots, expert_weight
 ):
-    code = jnp.where(route_slots < CAP, expert_ids * S + route_slots, -1)
-    pad = ((0, 0), (0, 8 - TOPK))
-    routes = jnp.concatenate(
-        [jnp.pad(code, pad, constant_values=-1), jnp.pad(gate_weights, pad)], axis=1
-    ).T
     up, lo, own, left, right = run(
-        upper_half, lower_half, upper_grad, lower_grad, routes, expert_weight
+        upper_half, lower_half, upper_grad, lower_grad,
+        expert_ids.T, gate_weights.T, route_slots.T, expert_weight,
     )
     weight_grad = own.astype(F32) + left.astype(F32) + right.astype(F32)
     return up, lo, weight_grad

time: 165 us -> 151 us (0.915)
  Pallas kernels: 154 us -> 142 us
  other arithmetic: 8.11 us -> 6.12 us
    pallas_call x1, Pallas kernels: 154 us -> 142 us  [run(): pl.pallas_call(kernel, out_shape=(rows, rows, half, half, half), in_specs...]
where the time goes in v2:
time: 151 us; the launch traced here: 150 us
  Pallas kernels  142 us (94%)
  other arithmetic  6.12 us (4%)
  local copies, waits for them, and re-layouts  1.59 us (1%)
    pallas_call x1, Pallas kernels, run(): pl.pallas_call(kernel, out_shape=(rows, rows, half, half, half), in_specs...  142 us
    add x1, other arithmetic, shards(): weight_grad = own.astype(F32) + left.astype(F32) + right.astype(F32)  6.12 us

profile of v2, /device:TPU:0, one launch (start us, length us, event | category | flops | bytes accessed | tf_op | source)
XLA Modules:
  0.0 150.3 jit_solution(4680265167603311394)
XLA Ops:
  0.6 141.9 %shard_map.103 = (bf16[128,2048]{1,0:T(8,128)(2,1)}, bf16[128,2048]{1,0:T(8,128)(2,1)}, bf16[2,256,2304]{2,1,0:T(8,128)(2,1)}, bf16[2,256,2304]{2,1,0:T(8,128)(2,1)}, bf16[2,256,2304]{2,1,0:T(8,128)(2,1)}) custom-call(bf16[128,2048]{1,0:T(8,128)(2,1)} %uh_in.1, bf16[128,2048]{1,0:T(8,128)(2,1)} %lh_in.1, bf16[128,2048]{1,0:T(8,128)(2,1)} %ug_in.1, ...), custom_call_target="tpu_custom_call" | custom-call | flops 28999999488 | bytes 30000000 | tf_op jit(solution)/shard_map/pallas_call | solution.py:515
  142.5 0.0 copy-start.1
  142.6 0.0 copy-start
  142.6 6.1 %convert_add_fusion = f32[2,256,2304]{2,1,0:T(8,128)} fusion(bf16[2,256,2304]{2,1,0:T(8,128)(2,1)} %get-tuple-element.12, bf16[2,256,2304]{2,1,0:T(8,128)(2,1)} %get-tuple-element.11, bf16[2,256,2304]{2,1,0:T(8,128)(2,1)} %get-tuple-element.10), kind=kLoop, calls=%fused_computation | loop fusion | flops 5898240 | bytes 11796480 | tf_op jit(solution)/shard_map/add | solution.py:573
  148.7 0.0 copy-done.1
  148.7 0.8 copy.13
  149.5 0.0 copy-done
  149.5 0.8 copy.14
Async XLA Ops:
  142.5 6.1 %copy-start.1 = (bf16[128,2048]{1,0:T(8,128)(2,1)S(1)}, bf16[128,2048]{1,0:T(8,128)(2,1)}, u32[]{:S(2)}) copy-start(bf16[128,2048]{1,0:T(8,128)(2,1)} %get-tuple-element.16) | copy-start | bytes 1572868
  142.6 6.9 %copy-start = (bf16[128,2048]{1,0:T(8,128)(2,1)S(1)}, bf16[128,2048]{1,0:T(8,128)(2,1)}, u32[]{:S(2)}) copy-start(bf16[128,2048]{1,0:T(8,128)(2,1)} %get-tuple-element.17) | copy-start | bytes 1572868

commit v3 on v2

--- a/solution.py
+++ b/solution.py
@@ -39,10 +39,10 @@
 
 def kernel(
     uh_in, lh_in, ug_in, lg_in, ids_in, gates_in, slots_in, w_hbm,
-    o_up, o_lo, o_own, o_left, o_right,
+    o_up, o_lo, o_sum, o_left, o_right,
     uh, lh, lg, ids, gates, slots_of, AG, RT, SD, R, O, W, G, PX, PG, OWN, TMP, FL, FR, FT,
     ag_s, ag_r, agf_s, agf_r, rt_s, rt_r, s2_s, s2_r, rb_s, rb_r,
-    px_s, px_r, pg_s, pg_r, x_s, x_r, fn_s, fn_r, loc, loc_b, w_sem, in_sem, credit, pcredit,
+    px_s, px_r, pg_s, pg_r, x_s, x_r, fn_s, fn_r, loc, loc_b, w_sem, in_sem, out_sem, credit, pcredit, xcredit,
 ):
     dp = lax.axis_index("dp")
     ex = lax.axis_index("expert")
@@ -70,7 +70,7 @@
         )
 
     def load_w(j):
-        return pltpu.make_async_copy(w_hbm.at[j], W, w_sem)
+        return pltpu.make_async_copy(w_hbm.at[j], W, w_sem.at[0])
 
     barrier = pltpu.get_barrier_semaphore()
     peers = [ydev(k) for k in (1, 2, 3)] + [zdev(k) for k in (1, 2, 3)] + [xdev(1), xdev(3), partner]
@@ -282,12 +282,12 @@
 
     def outputs_part(j, out, route):
         def tile(n, carry):
-            at = pl.ds(pl.multiple_of(n * 256, 256), 256)
+            at = pl.ds(pl.multiple_of(n * 512, 512), 512)
             out[:, at] = dot_nt(G[:, 2 * H :], W[at, 2 * H :]).astype(BF16)
             route[:, at] = dot_nt(G[:, : 2 * H], W[at, : 2 * H]).astype(BF16)
             return carry
 
-        lax.fori_loop(0, D // 256, tile, 0)
+        lax.fori_loop(0, D // 512, tile, 0)
 
     def weight_block(j, b, dst):
         mine = pl.ds(pl.multiple_of(b * 512 + c * SHARE, SHARE), SHARE)
@@ -295,7 +295,7 @@
 
         def tile(p, first, count):
             def body(n, carry):
-                at = pl.ds(pl.multiple_of(first + n * 256, 256), 256)
+                at = pl.ds(pl.multiple_of(first + n * H, H), H)
                 acc = dot_tn(R[p, j, :, mine], G[:, at])
                 acc = acc + dot_tn(PX[p, :, theirs], PG[:, at])
                 dst[:, at] = acc.astype(BF16)
@@ -303,8 +303,8 @@
 
             lax.fori_loop(0, count, body, 0)
 
-        tile(0, 0, 6)
-        tile(1, 2 * H, 3)
+        tile(0, 0, 2)
+        tile(1, 2 * H, 1)
 
     AH = pl.ds(0, SHARE // 2)
     BH = pl.ds(SHARE // 2, SHARE // 2)
@@ -313,14 +313,14 @@
         to = xdev(1 if d == 0 else 3)
         near = own((x + (1 if d == 0 else 3)) % RING)
         far = own((x + 2) % RING)
-        fin = o_left if d == 0 else o_right
         early, late = (AH, BH) if d == 0 else (BH, AH)
+        fin = (o_left, o_right)[d] if j == 0 else W.at[pl.ds((4 + d) * SHARE, SHARE)]
         if i == 0:
             src, dst = far.at[early], TMP.at[j, d]
         elif i == 1:
-            src, dst = near.at[late], fin.at[j, late]
+            src, dst = near.at[late], fin.at[late]
         else:
-            src, dst = near.at[early], fin.at[j, early]
+            src, dst = near.at[early], fin.at[early]
         return rcopy(src, dst, x_s.at[j, d, i], x_r.at[j, d, i], to)
 
     def weight_far(j, own):
@@ -352,10 +352,13 @@
             near[early, :] = (near[early, :].astype(F32) + TMP[j, d].astype(F32)).astype(BF16)
             x_copy(j, own, d, 2).start()
 
-    def x_done(j, own):
+    def x_arrived(j, own):
         for d in (0, 1):
             for i in (1, 2):
                 x_copy(j, own, d, i).wait_recv()
+
+    def x_sent(j, own):
+        for d in (0, 1):
             for i in range(3):
                 x_copy(j, own, d, i).wait_send()
 
@@ -410,20 +413,52 @@
     hidden_part(1)
     x_add(0, own0)
     outputs_part(1, O.at[0, 1], O.at[1, 1])
+    for k in (1, 3):
+        pl.semaphore_signal(xcredit, inc=1, device_id=xdev(k), device_id_type=MESH)
     pl.semaphore_wait(credit.at[1], 6)
     back(1, 0)
     weight_far(1, own1)
     back(1, 1)
+    pl.semaphore_wait(xcredit, 2)
     weight_near(1, own1, 0)
     back(1, 2)
     weight_near(1, own1, 1)
     back(1, 3)
     weight_own(1, own1)
     partner_sent()
-    own_copies = [pltpu.make_async_copy(own(x), o_own.at[j], w_sem) for j, own in enumerate((own0, own1))]
-    own_copies[0].start()
-    own_copies[0].wait()
-    own_copies[1].start()
+
+    pieces = [
+        pltpu.make_async_copy(src, G.at[pl.ds(d * SHARE, SHARE)], w_sem.at[1 + d])
+        for d, src in enumerate((o_left, o_right))
+    ]
+    sums = [
+        pltpu.make_async_copy(buf.at[pl.ds(0, SHARE)], o_sum.at[j], out_sem.at[j])
+        for j, buf in enumerate((G, PG))
+    ]
+
+    def fetch_pieces():
+        x_arrived(0, own0)
+        for piece in pieces:
+            piece.start()
+
+    def sum0():
+        for piece in pieces:
+            piece.wait()
+        G[0:SHARE, :] = (
+            own0(x)[...].astype(F32)
+            + G[0:SHARE, :].astype(F32)
+            + G[SHARE : 2 * SHARE, :].astype(F32)
+        ).astype(BF16)
+        sums[0].start()
+
+    def sum1():
+        x_arrived(1, own1)
+        PG[0:SHARE, :] = (
+            own1(x)[...].astype(F32)
+            + W[4 * SHARE : 5 * SHARE, :].astype(F32)
+            + W[5 * SHARE : 6 * SHARE, :].astype(F32)
+        ).astype(BF16)
+        sums[1].start()
 
     def fn_copy(p, d, i):
         to = a_dev[p](1 if d == 0 else 3)
@@ -477,22 +512,36 @@
                 fn_copy(p, 1, 0).start()
             elif i < 3:
                 fn_copy(p, i - 1, 1).start()
-
-    for p in (0, 1):
+        if i == 0:
+            fetch_pieces()
+        if i == 1:
+            sum0()
+
+    def fn_arrived(p):
         for d in (0, 1):
             for i in (1, 2):
                 fn_copy(p, d, i).wait_recv()
+
+    results = [
+        pltpu.make_async_copy(src, dst, out_sem.at[2 + p]) for p, (src, dst) in enumerate(((uh, o_up), (lg, o_lo)))
+    ]
     loads[5].wait()
     loads[6].wait()
+    low = lh[...].astype(F32)
+    scale = lax.rsqrt(jnp.mean(low * low, axis=1, keepdims=True) + NORM_EPS)
+    fn_arrived(0)
     mixture = AG[0, y].astype(F32) + FL[0].astype(F32) + FR[0].astype(F32)
-    o_up[...] = (uh[...].astype(F32) - mixture).astype(BF16)
+    uh[...] = (uh[...].astype(F32) - mixture).astype(BF16)
+    results[0].start()
+    fn_arrived(1)
     grad_normed = AG[1, z].astype(F32) + FL[1].astype(F32) + FR[1].astype(F32)
     low = lh[...].astype(F32)
-    scale = lax.rsqrt(jnp.mean(low * low, axis=1, keepdims=True) + NORM_EPS)
     inner = jnp.mean(low * grad_normed, axis=1, keepdims=True)
-    o_lo[...] = (
+    lg[...] = (
         lg[...].astype(F32) + scale * grad_normed - low * (scale * scale * scale) * inner
     ).astype(BF16)
+    results[1].start()
+    sum1()
 
     for p in (0, 1):
         for d in (0, 1):
@@ -501,22 +550,23 @@
         for j in (0, 1):
             for k in (1, 2, 3):
                 back_sent(p, j, k)
-    own_copies[1].wait()
-    x_done(0, own0)
-    x_done(1, own1)
+    x_sent(0, own0)
+    x_sent(1, own1)
+    for copy in results + sums:
+        copy.wait()
 
 
 def run(*arrays):
-    vm = pl.BlockSpec(memory_space=pltpu.VMEM)
     hbm = pl.BlockSpec(memory_space=pl.ANY)
     dma = pltpu.SemaphoreType.DMA
-    half = jax.ShapeDtypeStruct((2, SHARE, F), BF16)
+    half = jax.ShapeDtypeStruct((SHARE, F), BF16)
+    both = jax.ShapeDtypeStruct((2, SHARE, F), BF16)
     rows = jax.ShapeDtypeStruct((T, D), BF16)
     return pl.pallas_call(
         kernel,
-        out_shape=(rows, rows, half, half, half),
+        out_shape=(rows, rows, both, half, half),
         in_specs=[hbm] * 8,
-        out_specs=(vm, vm, hbm, hbm, hbm),
+        out_specs=(hbm,) * 5,
         scratch_shapes=[
             pltpu.VMEM((T, D), BF16),
             pltpu.VMEM((T, D), BF16),
@@ -549,9 +599,11 @@
             dma((2, 2, 3)), dma((2, 2, 3)),
             dma((2, 2)),
             dma((2, 2, 4)),
-            dma,
+            dma((3,)),
             dma((7,)),
+            dma((4,)),
             pltpu.SemaphoreType.REGULAR((2,)),
+            pltpu.SemaphoreType.REGULAR,
             pltpu.SemaphoreType.REGULAR,
         ],
         compiler_params=pltpu.CompilerParams(
@@ -566,12 +618,11 @@
 def shards(
     upper_half, lower_half, upper_grad, lower_grad, expert_ids, gate_weights, route_slots, expert_weight
 ):
-    up, lo, own, left, right = run(
+    up, lo, total, _, _ = run(
         upper_half, lower_half, upper_grad, lower_grad,
         expert_ids.T, gate_weights.T, route_slots.T, expert_weight,
     )
-    weight_grad = own.astype(F32) + left.astype(F32) + right.astype(F32)
-    return up, lo, weight_grad
+    return up, lo, total.astype(F32)
 
 
 def solution(mesh):

time: 151 us -> 146 us (0.967)
  Pallas kernels: 142 us -> 139 us
  other arithmetic: 6.12 us -> 4.27 us
    add x1 -> x0, other arithmetic: 6.12 us -> none  [shards(): weight_grad = own.astype(F32) + left.astype(F32) + right.astype(F32)]
    convert_element_type x0 -> x1, other arithmetic: none -> 4.27 us  [shards(): return (up, lo, total.astype(F32))]
    pallas_call x1, Pallas kernels: 142 us -> 139 us  [run(): pl.pallas_call(kernel, out_shape=(rows, rows, both, half, half), in_specs...]
where the time goes in v3:
time: 146 us
  Pallas kernels  139 us (95%)
  other arithmetic  4.27 us (3%)
  local copies, waits for them, and re-layouts  1.59 us (1%)
    pallas_call x1, Pallas kernels, run(): pl.pallas_call(kernel, out_shape=(rows, rows, both, half, half), in_specs...  139 us
    convert_element_type x1, other arithmetic, shards(): return (up, lo, total.astype(F32))  4.27 us

profile of v3, /device:TPU:0, one launch (start us, length us, event | category | flops | bytes accessed | tf_op | source)
XLA Modules:
  0.0 145.9 jit_solution(18331763743256223438)
XLA Ops:
  0.6 139.4 %shard_map.103 = (bf16[128,2048]{1,0:T(8,128)(2,1)}, bf16[128,2048]{1,0:T(8,128)(2,1)}, bf16[2,256,2304]{2,1,0:T(8,128)(2,1)}, bf16[256,2304]{1,0:T(8,128)(2,1)}, bf16[256,2304]{1,0:T(8,128)(2,1)}) custom-call(bf16[128,2048]{1,0:T(8,128)(2,1)} %uh_in.1, bf16[128,2048]{1,0:T(8,128)(2,1)} %lh_in.1, bf16[128,2048]{1,0:T(8,128)(2,1)} %ug_in.1, ...), custom_call_target="tpu_custom_call" | custom-call | flops 28999999488 | bytes 30000000 | tf_op jit(solution)/shard_map/pallas_call | solution.py:565
  140.0 0.0 copy-start.1
  140.0 0.0 copy-start
  140.1 4.3 %convert_element_type.3 = f32[2,256,2304]{2,1,0:T(8,128)} convert(bf16[2,256,2304]{2,1,0:T(8,128)(2,1)} %get-tuple-element.8) | non-fusion elementwise | flops 1179648 | bytes 7077888 | tf_op jit(solution)/shard_map/convert_element_type | solution.py:625
  144.3 0.0 copy-done.1
  144.3 0.8 copy.13
  145.1 0.0 copy-done
  145.1 0.8 copy.14
Async XLA Ops:
  140.0 4.3 %copy-start.1 = (bf16[128,2048]{1,0:T(8,128)(2,1)S(1)}, bf16[128,2048]{1,0:T(8,128)(2,1)}, u32[]{:S(2)}) copy-start(bf16[128,2048]{1,0:T(8,128)(2,1)} %get-tuple-element.12) | copy-start | bytes 1572868
  140.0 5.1 %copy-start = (bf16[128,2048]{1,0:T(8,128)(2,1)S(1)}, bf16[128,2048]{1,0:T(8,128)(2,1)}, u32[]{:S(2)}) copy-start(bf16[128,2048]{1,0:T(8,128)(2,1)} %get-tuple-element.13) | copy-start | bytes 1572868

commit v4 on v3

--- a/solution.py
+++ b/solution.py
@@ -39,10 +39,10 @@
 
 def kernel(
     uh_in, lh_in, ug_in, lg_in, ids_in, gates_in, slots_in, w_hbm,
-    o_up, o_lo, o_sum, o_left, o_right,
+    o_up, o_lo, o_sum, o_own, o_left, o_right,
     uh, lh, lg, ids, gates, slots_of, AG, RT, SD, R, O, W, G, PX, PG, OWN, TMP, FL, FR, FT,
     ag_s, ag_r, agf_s, agf_r, rt_s, rt_r, s2_s, s2_r, rb_s, rb_r,
-    px_s, px_r, pg_s, pg_r, x_s, x_r, fn_s, fn_r, loc, loc_b, w_sem, in_sem, out_sem, credit, pcredit, xcredit,
+    px_s, px_r, pg_s, pg_r, x_s, x_r, fn_s, fn_r, loc, loc_b, w_sem, in_sem, out_sem, credit, pcredit,
 ):
     dp = lax.axis_index("dp")
     ex = lax.axis_index("expert")
@@ -314,7 +314,7 @@
         near = own((x + (1 if d == 0 else 3)) % RING)
         far = own((x + 2) % RING)
         early, late = (AH, BH) if d == 0 else (BH, AH)
-        fin = (o_left, o_right)[d] if j == 0 else W.at[pl.ds((4 + d) * SHARE, SHARE)]
+        fin = (o_left, o_right)[d].at[j]
         if i == 0:
             src, dst = far.at[early], TMP.at[j, d]
         elif i == 1:
@@ -413,13 +413,10 @@
     hidden_part(1)
     x_add(0, own0)
     outputs_part(1, O.at[0, 1], O.at[1, 1])
-    for k in (1, 3):
-        pl.semaphore_signal(xcredit, inc=1, device_id=xdev(k), device_id_type=MESH)
     pl.semaphore_wait(credit.at[1], 6)
     back(1, 0)
     weight_far(1, own1)
     back(1, 1)
-    pl.semaphore_wait(xcredit, 2)
     weight_near(1, own1, 0)
     back(1, 2)
     weight_near(1, own1, 1)
@@ -427,14 +424,13 @@
     weight_own(1, own1)
     partner_sent()
 
+    own_out = pltpu.make_async_copy(own1(x), o_own, out_sem.at[1])
+    own_out.start()
     pieces = [
-        pltpu.make_async_copy(src, G.at[pl.ds(d * SHARE, SHARE)], w_sem.at[1 + d])
+        pltpu.make_async_copy(src.at[0], G.at[pl.ds(d * SHARE, SHARE)], w_sem.at[1 + d])
         for d, src in enumerate((o_left, o_right))
     ]
-    sums = [
-        pltpu.make_async_copy(buf.at[pl.ds(0, SHARE)], o_sum.at[j], out_sem.at[j])
-        for j, buf in enumerate((G, PG))
-    ]
+    sum_out = pltpu.make_async_copy(G.at[pl.ds(0, SHARE)], o_sum, out_sem.at[0])
 
     def fetch_pieces():
         x_arrived(0, own0)
@@ -449,16 +445,7 @@
             + G[0:SHARE, :].astype(F32)
             + G[SHARE : 2 * SHARE, :].astype(F32)
         ).astype(BF16)
-        sums[0].start()
-
-    def sum1():
-        x_arrived(1, own1)
-        PG[0:SHARE, :] = (
-            own1(x)[...].astype(F32)
-            + W[4 * SHARE : 5 * SHARE, :].astype(F32)
-            + W[5 * SHARE : 6 * SHARE, :].astype(F32)
-        ).astype(BF16)
-        sums[1].start()
+        sum_out.start()
 
     def fn_copy(p, d, i):
         to = a_dev[p](1 if d == 0 else 3)
@@ -541,7 +528,7 @@
         lg[...].astype(F32) + scale * grad_normed - low * (scale * scale * scale) * inner
     ).astype(BF16)
     results[1].start()
-    sum1()
+    x_arrived(1, own1)
 
     for p in (0, 1):
         for d in (0, 1):
@@ -552,7 +539,7 @@
                 back_sent(p, j, k)
     x_sent(0, own0)
     x_sent(1, own1)
-    for copy in results + sums:
+    for copy in results + [own_out, sum_out]:
         copy.wait()
 
 
@@ -564,9 +551,9 @@
     rows = jax.ShapeDtypeStruct((T, D), BF16)
     return pl.pallas_call(
         kernel,
-        out_shape=(rows, rows, both, half, half),
+        out_shape=(rows, rows, half, half, both, both),
         in_specs=[hbm] * 8,
-        out_specs=(hbm,) * 5,
+        out_specs=(hbm,) * 6,
         scratch_shapes=[
             pltpu.VMEM((T, D), BF16),
             pltpu.VMEM((T, D), BF16),
@@ -604,7 +591,6 @@
             dma((4,)),
             pltpu.SemaphoreType.REGULAR((2,)),
             pltpu.SemaphoreType.REGULAR,
-            pltpu.SemaphoreType.REGULAR,
         ],
         compiler_params=pltpu.CompilerParams(
             collective_id=0, has_side_effects=True, vmem_limit_bytes=63 * 1024 * 1024
@@ -615,14 +601,51 @@
     )(*arrays)
 
 
+STEPS = 8
+
+
+def finish_kernel(up, lo, total, own, left, right, o_up, o_lo, o_weight):
+    o_up[...] = up[...]
+    o_lo[...] = lo[...]
+    i = pl.program_id(0)
+
+    @pl.when(i < STEPS // 2)
+    def _():
+        o_weight[0] = total[...].astype(F32)
+
+    @pl.when(i >= STEPS // 2)
+    def _():
+        o_weight[0] = own[...].astype(F32) + left[0].astype(F32) + right[0].astype(F32)
+
+
+def finish(*arrays):
+    per = STEPS // 2
+    tall = 2 * SHARE // STEPS
+    row = pl.BlockSpec((T // STEPS, D), lambda i: (i, 0))
+    first = pl.BlockSpec((tall, F), lambda i: (jnp.minimum(i, per - 1), 0))
+    second = pl.BlockSpec((tall, F), lambda i: (jnp.maximum(i - per, 0), 0))
+    piece = pl.BlockSpec((1, tall, F), lambda i: (1, jnp.maximum(i - per, 0), 0))
+    return pl.pallas_call(
+        finish_kernel,
+        out_shape=(
+            jax.ShapeDtypeStruct((T, D), BF16),
+            jax.ShapeDtypeStruct((T, D), BF16),
+            jax.ShapeDtypeStruct((2, SHARE, F), F32),
+        ),
+        grid=(STEPS,),
+        in_specs=[row, row, first, second, piece, piece],
+        out_specs=(row, row, pl.BlockSpec((1, tall, F), lambda i: (i // per, i % per, 0))),
+        cost_estimate=pl.CostEstimate(flops=3_000_000, bytes_accessed=11_500_000, transcendentals=0),
+    )(*arrays)
+
+
 def shards(
     upper_half, lower_half, upper_grad, lower_grad, expert_ids, gate_weights, route_slots, expert_weight
 ):
-    up, lo, total, _, _ = run(
+    return finish(*run(
         upper_half, lower_half, upper_grad, lower_grad,
         expert_ids.T, gate_weights.T, route_slots.T, expert_weight,
-    )
-    return up, lo, total.astype(F32)
+    ))
 
 
 def solution(mesh):

time: 146 us -> 147 us (level)
  Pallas kernels: 139 us -> 146 us
  other arithmetic: 4.27 us -> 0 us
  local copies, waits for them, and re-layouts: 1.59 us -> 0 us
    pallas_call x1 -> x2, Pallas kernels: 139 us -> 146 us  [the longest x1 138 us: run(): pl.pallas_call(kernel, out_shape=(rows, rows, half, half, both, both), in...]
    convert_element_type x1 -> x0, other arithmetic: 4.27 us -> none  [shards(): return (up, lo, total.astype(F32))]
    unnamed x6 -> x0, local copies, waits for them, and re-layouts: 1.59 us -> none
where the time goes in v4:
time: 147 us; the launch traced here: 146 us
  Pallas kernels  146 us (99%)
    pallas_call x1, Pallas kernels, run(): pl.pallas_call(kernel, out_shape=(rows, rows, half, half, both, both), in...  138 us
    pallas_call x1, Pallas kernels, finish(): pl.pallas_call(finish_kernel, out_shape=(jax.ShapeDtypeStruct((T, D), BF1...  7.57 us

profile of v4, /device:TPU:0, one launch (start us, length us, event | category | flops | bytes accessed | tf_op | source)
XLA Modules:
  0.0 146.4 jit_solution(465864828417199832)
XLA Ops:
  0.6 138.2 %shard_map.103 = (bf16[128,2048]{1,0:T(8,128)(2,1)}, bf16[128,2048]{1,0:T(8,128)(2,1)}, bf16[256,2304]{1,0:T(8,128)(2,1)}, bf16[256,2304]{1,0:T(8,128)(2,1)}, bf...) custom-call(bf16[128,2048]{1,0:T(8,128)(2,1)} %uh_in.1, bf16[128,2048]{1,0:T(8,128)(2,1)} %lh_in.1, ...), custom_call_target="tpu_custom_call" | custom-call | flops 28999999488 | bytes 30000000 | tf_op jit(solution)/shard_map/pallas_call | solution.py:552
  138.8 7.6 %shard_map.104 = (bf16[128,2048]{1,0:T(8,128)(2,1)}, bf16[128,2048]{1,0:T(8,128)(2,1)}, f32[2,256,2304]{2,1,0:T(8,128)}) custom-call(bf16[128,2048]{1,0:T(8,128)(2,1)} %get-tuple-element.9.up, bf16[128,2048]{1,0:T(8,128)(2,1)} %get-tuple-element.10.lo, bf16[256,2304]{1,0:T(8,128)(2,1)} %get-tuple-element.11.total, bf16[256,2304]{1,0:T(8,128)(2,1)} %get-tuple-element.12.own, ...), custom_call_target="tpu_custom_call" | custom-call | flops 3000000 | bytes 11500000 | tf_op jit(solution)/shard_map/pallas_call | solution.py:628

commit v5 on v4

--- a/solution.py
+++ b/solution.py
@@ -601,30 +601,38 @@
     )(*arrays)
 
 
-STEPS = 8
-
-
-def finish_kernel(up, lo, total, own, left, right, o_up, o_lo, o_weight):
-    o_up[...] = up[...]
-    o_lo[...] = lo[...]
-    i = pl.program_id(0)
-
-    @pl.when(i < STEPS // 2)
-    def _():
-        o_weight[0] = total[...].astype(F32)
-
-    @pl.when(i >= STEPS // 2)
-    def _():
-        o_weight[0] = own[...].astype(F32) + left[0].astype(F32) + right[0].astype(F32)
+def finish_kernel(up, lo, total, own, left, right, o_up, o_lo, o_weight, parts, wide, pass_sem, in_sem, out_sem):
+    half = SHARE // 2
+    loads = []
+    for q in range(4):
+        at = pl.ds((q % 2) * half, half)
+        srcs = (total.at[at],) if q < 2 else (own.at[at], left.at[1, at], right.at[1, at])
+        loads.append([
+            pltpu.make_async_copy(src, parts.at[q, i], in_sem.at[q, i]) for i, src in enumerate(srcs)
+        ])
+    passed = [
+        pltpu.make_async_copy(src, dst, pass_sem.at[i]) for i, (src, dst) in enumerate(((up, o_up), (lo, o_lo)))
+    ]
+    for load in loads[0] + loads[1] + loads[2] + loads[3] + passed:
+        load.start()
+    stores = []
+    for q in range(4):
+        for load in loads[q]:
+            load.wait()
+        value = parts[q, 0].astype(F32)
+        if q >= 2:
+            value = value + parts[q, 1].astype(F32) + parts[q, 2].astype(F32)
+        wide[q] = value
+        store = pltpu.make_async_copy(wide.at[q], o_weight.at[q // 2, pl.ds((q % 2) * half, half)], out_sem.at[q])
+        store.start()
+        stores.append(store)
+    for copy in passed + stores:
+        copy.wait()
 
 
 def finish(*arrays):
-    per = STEPS // 2
-    tall = 2 * SHARE // STEPS
-    row = pl.BlockSpec((T // STEPS, D), lambda i: (i, 0))
-    first = pl.BlockSpec((tall, F), lambda i: (jnp.minimum(i, per - 1), 0))
-    second = pl.BlockSpec((tall, F), lambda i: (jnp.maximum(i - per, 0), 0))
-    piece = pl.BlockSpec((1, tall, F), lambda i: (1, jnp.maximum(i - per, 0), 0))
+    hbm = pl.BlockSpec(memory_space=pl.ANY)
+    dma = pltpu.SemaphoreType.DMA
     return pl.pallas_call(
         finish_kernel,
         out_shape=(
@@ -632,9 +640,14 @@
             jax.ShapeDtypeStruct((T, D), BF16),
             jax.ShapeDtypeStruct((2, SHARE, F), F32),
         ),
-        grid=(STEPS,),
-        in_specs=[row, row, first, second, piece, piece],
-        out_specs=(row, row, pl.BlockSpec((1, tall, F), lambda i: (i // per, i % per, 0))),
+        in_specs=[hbm] * 6,
+        out_specs=(hbm,) * 3,
+        scratch_shapes=[
+            pltpu.VMEM((4, 3, SHARE // 2, F), BF16),
+            pltpu.VMEM((4, SHARE // 2, F), F32),
+            dma((2,)), dma((4, 3)), dma((4,)),
+        ],
+        compiler_params=pltpu.CompilerParams(vmem_limit_bytes=60 * 1024 * 1024),
         cost_estimate=pl.CostEstimate(flops=3_000_000, bytes_accessed=11_500_000, transcendentals=0),
     )(*arrays)
 

time: 147 us -> 172 us (1.17)
  Pallas kernels: 146 us -> 171 us
    pallas_call x1, Pallas kernels: 7.57 us -> 33 us  [finish(): pl.pallas_call(finish_kernel, out_shape=(jax.ShapeDtypeStruct((T, D), BF1...]
where the time goes in v5:
time: 172 us
  Pallas kernels  171 us (99%)
    pallas_call x1, Pallas kernels, run(): pl.pallas_call(kernel, out_shape=(rows, rows, half, half, both, both), in...  138 us
    pallas_call x1, Pallas kernels, finish(): pl.pallas_call(finish_kernel, out_shape=(jax.ShapeDtypeStruct((T, D), BF1...  33 us

profile of v5, /device:TPU:0, one launch (start us, length us, event | category | flops | bytes accessed | tf_op | source)
XLA Modules:
  0.0 172.0 jit_solution(8770790475584854355)
XLA Ops:
  0.6 138.2 %shard_map.103 = (bf16[128,2048]{1,0:T(8,128)(2,1)}, bf16[128,2048]{1,0:T(8,128)(2,1)}, bf16[256,2304]{1,0:T(8,128)(2,1)}, bf16[256,2304]{1,0:T(8,128)(2,1)}, bf...) custom-call(bf16[128,2048]{1,0:T(8,128)(2,1)} %uh_in.1, bf16[128,2048]{1,0:T(8,128)(2,1)} %lh_in.1, ...), custom_call_target="tpu_custom_call" | custom-call | flops 28999999488 | bytes 30000000 | tf_op jit(solution)/shard_map/pallas_call | solution.py:552
  138.8 33.0 %shard_map.104 = (bf16[128,2048]{1,0:T(8,128)(2,1)}, bf16[128,2048]{1,0:T(8,128)(2,1)}, f32[2,256,2304]{2,1,0:T(8,128)}) custom-call(bf16[128,2048]{1,0:T(8,128)(2,1)} %get-tuple-element.9.up, bf16[128,2048]{1,0:T(8,128)(2,1)} %get-tuple-element.10.lo, bf16[256,2304]{1,0:T(8,128)(2,1)} %get-tuple-element.11.total, bf16[256,2304]{1,0:T(8,128)(2,1)} %get-tuple-element.12.own, ...), custom_call_target="tpu_custom_call" | custom-call | flops 3000000 | bytes 11500000 | tf_op jit(solution)/shard_map/pallas_call | solution.py:636

commit v6 on v5

--- a/solution.py
+++ b/solution.py
@@ -601,7 +601,7 @@
     )(*arrays)
 
 
-def finish_kernel(up, lo, total, own, left, right, o_up, o_lo, o_weight, parts, wide, pass_sem, in_sem, out_sem):
+def finish_kernel(up, lo, total, own, left, right, o_up, o_lo, o_weight, parts, wide, tok, tok_sem, in_sem, out_sem):
     half = SHARE // 2
     loads = []
     for q in range(4):
@@ -610,10 +610,9 @@
         loads.append([
             pltpu.make_async_copy(src, parts.at[q, i], in_sem.at[q, i]) for i, src in enumerate(srcs)
         ])
-    passed = [
-        pltpu.make_async_copy(src, dst, pass_sem.at[i]) for i, (src, dst) in enumerate(((up, o_up), (lo, o_lo)))
-    ]
-    for load in loads[0] + loads[1] + loads[2] + loads[3] + passed:
+    fetched = [pltpu.make_async_copy(src, tok.at[i], tok_sem.at[i, 0]) for i, src in enumerate((up, lo))]
+    passed = [pltpu.make_async_copy(tok.at[i], dst, tok_sem.at[i, 1]) for i, dst in enumerate((o_up, o_lo))]
+    for load in loads[0] + fetched + loads[1] + loads[2] + loads[3]:
         load.start()
     stores = []
     for q in range(4):
@@ -626,6 +625,9 @@
         store = pltpu.make_async_copy(wide.at[q], o_weight.at[q // 2, pl.ds((q % 2) * half, half)], out_sem.at[q])
         store.start()
         stores.append(store)
+        if q < 2:
+            fetched[q].wait()
+            passed[q].start()
     for copy in passed + stores:
         copy.wait()
 
@@ -645,7 +647,8 @@
         scratch_shapes=[
             pltpu.VMEM((4, 3, SHARE // 2, F), BF16),
             pltpu.VMEM((4, SHARE // 2, F), F32),
-            dma((2,)), dma((4, 3)), dma((4,)),
+            pltpu.VMEM((2, T, D), BF16),
+            dma((2, 2)), dma((4, 3)), dma((4,)),
         ],
         compiler_params=pltpu.CompilerParams(vmem_limit_bytes=60 * 1024 * 1024),
         cost_estimate=pl.CostEstimate(flops=3_000_000, bytes_accessed=11_500_000, transcendentals=0),

time: 172 us -> 144 us (0.84)
  Pallas kernels: 171 us -> 143 us
    pallas_call x1, Pallas kernels: 33 us -> 4.65 us  [finish(): pl.pallas_call(finish_kernel, out_shape=(jax.ShapeDtypeStruct((T, D), BF1...]
where the time goes in v6:
time: 144 us
  Pallas kernels  143 us (99%)
    pallas_call x1, Pallas kernels, run(): pl.pallas_call(kernel, out_shape=(rows, rows, half, half, both, both), in...  138 us
    pallas_call x1, Pallas kernels, finish(): pl.pallas_call(finish_kernel, out_shape=(jax.ShapeDtypeStruct((T, D), BF1...  4.65 us

profile of v6, /device:TPU:0, one launch (start us, length us, event | category | flops | bytes accessed | tf_op | source)
XLA Modules:
  0.0 143.6 jit_solution(11258071872229578673)
XLA Ops:
  0.6 138.2 %shard_map.103 = (bf16[128,2048]{1,0:T(8,128)(2,1)}, bf16[128,2048]{1,0:T(8,128)(2,1)}, bf16[256,2304]{1,0:T(8,128)(2,1)}, bf16[256,2304]{1,0:T(8,128)(2,1)}, bf...) custom-call(bf16[128,2048]{1,0:T(8,128)(2,1)} %uh_in.1, bf16[128,2048]{1,0:T(8,128)(2,1)} %lh_in.1, ...), custom_call_target="tpu_custom_call" | custom-call | flops 28999999488 | bytes 30000000 | tf_op jit(solution)/shard_map/pallas_call | solution.py:552
  138.8 4.6 %shard_map.104 = (bf16[128,2048]{1,0:T(8,128)(2,1)}, bf16[128,2048]{1,0:T(8,128)(2,1)}, f32[2,256,2304]{2,1,0:T(8,128)}) custom-call(bf16[128,2048]{1,0:T(8,128)(2,1)} %get-tuple-element.9.up, bf16[128,2048]{1,0:T(8,128)(2,1)} %get-tuple-element.10.lo, bf16[256,2304]{1,0:T(8,128)(2,1)} %get-tuple-element.11.total, bf16[256,2304]{1,0:T(8,128)(2,1)} %get-tuple-element.12.own, ...), custom_call_target="tpu_custom_call" | custom-call | flops 3000000 | bytes 11500000 | tf_op jit(solution)/shard_map/pallas_call | solution.py:638

commit v7 on v6

--- a/solution.py
+++ b/solution.py
@@ -20,6 +20,8 @@
 TOPK = 6
 CAP = 30
 S = 32
+EARLY = 2
+LATE = 4 * (CAP - EARLY)
 M = 16 * S
 RING = 4
 SHARE = D // 8
@@ -96,6 +98,10 @@
     AG[0, y] = (low * scale).astype(BF16)
     loads[1].wait()
 
+    for p in (0, 1):
+        for line in range(RING):
+            O[p, 1, line * T + LATE : (line + 1) * T, :] = jnp.zeros((T - LATE, D), BF16)
+
     pl.semaphore_wait(barrier, len(peers))
 
     HALF = T // 2
@@ -129,14 +135,16 @@
 
     row = lax.broadcasted_iota(jnp.int32, (T, T), 0)
 
-    def codes_of(p, j):
+    def codes_of(p, j, filled=False):
         b, s = row >> 5, row & 31
+        if filled:
+            s = jnp.where(s < CAP, s, s + S - EARLY)
         if p == 0:
             return 64 * (4 * y + b) + 32 * j + s
         return 64 * (4 * b + z) + 32 * j + s
 
-    def onehot(p, j, a):
-        val = codes_of(p, j)
+    def onehot(p, j, a, filled=False):
+        val = codes_of(p, j, filled)
         hot = jnp.zeros((T, T), F32)
         share = jnp.zeros((T, T), F32)
         for k in range(TOPK):
@@ -147,7 +155,7 @@
         return hot, share
 
     def gather(p, j, a):
-        hot, share = onehot(p, j, a)
+        hot, share = onehot(p, j, a, True)
         hot = hot.astype(BF16)
         for n in range(4):
             cols = pl.ds(n * 512, 512)
@@ -178,11 +186,75 @@
             SD.at[p, j, a, slots(b_me[p])], R.at[p, j, r_rows(p, a)], loc.at[p, j]
         ).start()
 
+    def raw(p, line):
+        return O.at[p, 1, pl.ds(pl.multiple_of(line * T, T), LATE)]
+
     def s2_whole(p, j, k):
-        return rcopy(SD.at[p, j, 0], R.at[p, j, pl.ds(0, T)], s2_s.at[p, j, k], s2_r.at[p, j, k], b_dev[p](k))
+        if j == 0:
+            src, dst = SD.at[p, j, 0], R.at[p, j, pl.ds(0, T)]
+        else:
+            src, dst = SD.at[p, j, (b_me[p] + k) % RING, pl.ds(0, LATE)], raw(p, b_me[p])
+        return rcopy(src, dst, s2_s.at[p, j, k], s2_r.at[p, j, k], b_dev[p](k))
 
     def loc_whole(p, j):
-        return pltpu.make_async_copy(SD.at[p, j, 0], R.at[p, j, pl.ds(0, T)], loc.at[p, j])
+        if j == 0:
+            src, dst = SD.at[p, j, 0], R.at[p, j, pl.ds(0, T)]
+        else:
+            src, dst = SD.at[p, j, b_me[p], pl.ds(0, LATE)], raw(p, b_me[p])
+        return pltpu.make_async_copy(src, dst, loc.at[p, j])
+
+    def gather_late(p):
+        shape = (RING * LATE, T)
+        r = lax.broadcasted_iota(jnp.int32, shape, 0)
+
+        def over(v, step):
+            return sum((v >= step * i).astype(jnp.int32) for i in (1, 2, 3))
+
+        b = over(r, LATE)
+        r = r - LATE * b
+        owner = over(r, CAP - EARLY)
+        s = r - (CAP - EARLY) * owner
+        val = 64 * (4 * y + b if p == 0 else 4 * b + z) + S + s
+        share = jnp.zeros(shape, F32)
+        hots = []
+        for a in range(RING):
+            mine = jnp.where(owner == a, val, -2)
+            hot = jnp.zeros(shape, F32)
+            for k in range(TOPK):
+                m = RT[p, a, k : k + 1, :] == mine
+                hot = jnp.where(m, 1.0, hot)
+                if p == 1:
+                    gate = RT[p, a, 8 + k : 9 + k, :].astype(F32) * (1.0 / GATE_DENOM)
+                    share = jnp.where(m, gate, share)
+            hots.append(hot.astype(BF16))
+        for n in range(4):
+            cols = pl.ds(n * 512, 512)
+            picked = jnp.zeros((RING * LATE, 512), F32)
+            for a in range(RING):
+                picked = picked + dot_nn(hots[a], AG[p, a, :, cols])
+            if p == 1:
+                picked = picked * jnp.sum(share, axis=1, keepdims=True)
+            for b in range(RING):
+                SD[p, 1, b, 0:LATE, cols] = picked[b * LATE : (b + 1) * LATE].astype(BF16)
+
+    def unpack():
+        r = lax.broadcasted_iota(jnp.int32, (T, T), 0)
+        q = lax.broadcasted_iota(jnp.int32, (T, T), 1)
+        s = r & 31
+        sent = (s < CAP - EARLY) & (q == (r >> 5) * (CAP - EARLY) + s)
+        early = (s >= CAP - EARLY) & (s < CAP) & (q == r + EARLY)
+        sent = jnp.where(sent, 1.0, 0.0).astype(BF16)
+        early = jnp.where(early, 1.0, 0.0).astype(BF16)
+        for p in (0, 1):
+            for line in range(RING):
+                blocks = [(a * RING + line if p == 0 else line * RING + a) * S for a in range(RING)]
+                for n in range(4):
+                    cols = pl.ds(n * 512, 512)
+                    first = jnp.concatenate([R[p, 0, i : i + S, cols] for i in blocks], axis=0)
+                    value = dot_nn(sent, O[p, 1, line * T : (line + 1) * T, cols]) + dot_nn(early, first)
+                    value = value.astype(BF16)
+                    for a, i in enumerate(blocks):
+                        R[p, 1, i : i + S, cols] = value[a * S : (a + 1) * S]
 
     for p in (1, 0):
         gather(p, 0, a_me[p])
@@ -208,12 +280,8 @@
         gather(p, 0, (a_me[p] + 2) % RING)
         s2_send(p, 0, (a_me[p] + 2) % RING)
 
-    def gather_later(a, carry):
-        for p in (1, 0):
-            gather(p, 1, a)
-        return carry
-
-    lax.fori_loop(0, RING, gather_later, 0)
+    for p in (1, 0):
+        gather_late(p)
     for p in (1, 0):
         for k in (1, 2, 3):
             rt_copy(p, k).wait_send()
@@ -233,12 +301,10 @@
 
     s2_sent(0)
 
-    def send_later(a, carry):
-        for p in (1, 0):
-            s2_send(p, 1, a)
-        return carry
-
-    lax.fori_loop(0, RING, send_later, 0)
+    for p in (1, 0):
+        for k in (1, 2, 3):
+            s2_whole(p, 1, k).start()
+        loc_whole(p, 1).start()
 
     def px_copy(p, j, b):
         src = R.at[p, j, :, pl.ds(pl.multiple_of(b * 512 + (1 - c) * SHARE, SHARE), SHARE)]
@@ -258,6 +324,7 @@
             for k in (1, 2, 3):
                 s2_whole(p, j, k).wait_recv()
         if j == 1:
+            unpack()
             pl.semaphore_wait(pcredit, 1)
         for p in (0, 1):
             for b in range(RING):
@@ -271,9 +338,12 @@
             grad = dot_nn(R[1, j], W[:, at[2]])
             sig = jax.nn.sigmoid(gate)
             act = gate * sig
-            G[:, at[2]] = (act * up).astype(BF16)
-            G[:, at[0]] = (grad * up * sig * (1.0 + gate * (1.0 - sig))).astype(BF16)
-            G[:, at[1]] = (grad * act).astype(BF16)
+            parts = (grad * up * sig * (1.0 + gate * (1.0 - sig)), grad * act, act * up)
+            if j == 0:
+                live = (lax.broadcasted_iota(jnp.int32, (M, 256), 0) & 31) < CAP
+                parts = [jnp.where(live, part, 0.0) for part in parts]
+            for i in range(3):
+                G[:, at[i]] = parts[i].astype(BF16)
             for i in range(3):
                 pg_copy(at[i]).start()
             return carry

time: 144 us -> 148 us (1.028)
  the two profiles are of different devices: /device:TPU:0 before, /device:TPU:121 now
where the time goes in v7:
time: 148 us
  Pallas kernels  147 us (99%)
    pallas_call x1, Pallas kernels, run(): pl.pallas_call(kernel, out_shape=(rows, rows, half, half, both, both), in...  142 us
    pallas_call x1, Pallas kernels, finish(): pl.pallas_call(finish_kernel, out_shape=(jax.ShapeDtypeStruct((T, D), BF1...  4.65 us

profile of v7, /device:TPU:121, one launch (start us, length us, event | category | flops | bytes accessed | tf_op | source)
XLA Modules:
  0.0 148.0 jit_solution(334523910933486301)
XLA Ops:
  0.6 142.5 %shard_map.103 = (bf16[128,2048]{1,0:T(8,128)(2,1)}, bf16[128,2048]{1,0:T(8,128)(2,1)}, bf16[256,2304]{1,0:T(8,128)(2,1)}, bf16[256,2304]{1,0:T(8,128)(2,1)}, bf...) custom-call(bf16[128,2048]{1,0:T(8,128)(2,1)} %uh_in.1, bf16[128,2048]{1,0:T(8,128)(2,1)} %lh_in.1, ...), custom_call_target="tpu_custom_call" | custom-call | flops 28999999488 | bytes 30000000 | tf_op jit(solution)/shard_map/pallas_call | solution.py:622
  143.1 4.6 %shard_map.104 = (bf16[128,2048]{1,0:T(8,128)(2,1)}, bf16[128,2048]{1,0:T(8,128)(2,1)}, f32[2,256,2304]{2,1,0:T(8,128)}) custom-call(bf16[128,2048]{1,0:T(8,128)(2,1)} %get-tuple-element.9.up, bf16[128,2048]{1,0:T(8,128)(2,1)} %get-tuple-element.10.lo, bf16[256,2304]{1,0:T(8,128)(2,1)} %get-tuple-element.11.total, bf16[256,2304]{1,0:T(8,128)(2,1)} %get-tuple-element.12.own, ...), custom_call_target="tpu_custom_call" | custom-call | flops 3000000 | bytes 11500000 | tf_op jit(solution)/shard_map/pallas_call | solution.py:708

commit v8 on v6

--- a/solution.py
+++ b/solution.py
@@ -82,9 +82,8 @@
         (uh_in, uh), (lg_in, lg),
     )
     loads = [pltpu.make_async_copy(src, dst, in_sem.at[i]) for i, (src, dst) in enumerate(pairs)]
-    for load in loads:
+    for load in loads[:5]:
         load.start()
-    load_w(0).start()
     for i in (2, 3, 4):
         loads[i].wait()
     for p in (0, 1):
@@ -126,6 +125,9 @@
     for p in (1, 0):
         ag_copy(p, 0, 1).start()
         ag_copy(p, 1, 0).start()
+    for load in loads[5:]:
+        load.start()
+    load_w(0).start()
 
     row = lax.broadcasted_iota(jnp.int32, (T, T), 0)
 
@@ -601,28 +603,32 @@
     )(*arrays)
 
 
+PIECES = 8
+
+
 def finish_kernel(up, lo, total, own, left, right, o_up, o_lo, o_weight, parts, wide, tok, tok_sem, in_sem, out_sem):
-    half = SHARE // 2
+    per = PIECES // 2
+    tall = SHARE // per
     loads = []
-    for q in range(4):
-        at = pl.ds((q % 2) * half, half)
-        srcs = (total.at[at],) if q < 2 else (own.at[at], left.at[1, at], right.at[1, at])
+    for q in range(PIECES):
+        at = pl.ds((q % per) * tall, tall)
+        srcs = (total.at[at],) if q < per else (own.at[at], left.at[1, at], right.at[1, at])
         loads.append([
             pltpu.make_async_copy(src, parts.at[q, i], in_sem.at[q, i]) for i, src in enumerate(srcs)
         ])
     fetched = [pltpu.make_async_copy(src, tok.at[i], tok_sem.at[i, 0]) for i, src in enumerate((up, lo))]
     passed = [pltpu.make_async_copy(tok.at[i], dst, tok_sem.at[i, 1]) for i, dst in enumerate((o_up, o_lo))]
-    for load in loads[0] + fetched + loads[1] + loads[2] + loads[3]:
+    for load in loads[0] + fetched + sum(loads[1:], []):
         load.start()
     stores = []
-    for q in range(4):
+    for q in range(PIECES):
         for load in loads[q]:
             load.wait()
         value = parts[q, 0].astype(F32)
-        if q >= 2:
+        if q >= per:
             value = value + parts[q, 1].astype(F32) + parts[q, 2].astype(F32)
         wide[q] = value
-        store = pltpu.make_async_copy(wide.at[q], o_weight.at[q // 2, pl.ds((q % 2) * half, half)], out_sem.at[q])
+        store = pltpu.make_async_copy(wide.at[q], o_weight.at[q // per, pl.ds((q % per) * tall, tall)], out_sem.at[q])
         store.start()
         stores.append(store)
         if q < 2:
@@ -645,10 +651,10 @@
         in_specs=[hbm] * 6,
         out_specs=(hbm,) * 3,
         scratch_shapes=[
-            pltpu.VMEM((4, 3, SHARE // 2, F), BF16),
-            pltpu.VMEM((4, SHARE // 2, F), F32),
+            pltpu.VMEM((PIECES, 3, 2 * SHARE // PIECES, F), BF16),
+            pltpu.VMEM((PIECES, 2 * SHARE // PIECES, F), F32),
             pltpu.VMEM((2, T, D), BF16),
-            dma((2, 2)), dma((4, 3)), dma((4,)),
+            dma((2, 2)), dma((PIECES, 3)), dma((PIECES,)),
         ],
         compiler_params=pltpu.CompilerParams(vmem_limit_bytes=60 * 1024 * 1024),
         cost_estimate=pl.CostEstimate(flops=3_000_000, bytes_accessed=11_500_000, transcendentals=0),

time: 144 us -> 144 us (level)
  no operation moved by 1% of the time
where the time goes in v8:
time: 144 us
  Pallas kernels  143 us (99%)
    pallas_call x1, Pallas kernels, run(): pl.pallas_call(kernel, out_shape=(rows, rows, half, half, both, both), in...  138 us
    pallas_call x1, Pallas kernels, finish(): pl.pallas_call(finish_kernel, out_shape=(jax.ShapeDtypeStruct((T, D), BF1...  5.14 us

profile of v8, /device:TPU:0, one launch (start us, length us, event | category | flops | bytes accessed | tf_op | source)
XLA Modules:
  0.0 144.1 jit_solution(6885758621633626025)
XLA Ops:
  0.6 138.2 %shard_map.103 = (bf16[128,2048]{1,0:T(8,128)(2,1)}, bf16[128,2048]{1,0:T(8,128)(2,1)}, bf16[256,2304]{1,0:T(8,128)(2,1)}, bf16[256,2304]{1,0:T(8,128)(2,1)}, bf...) custom-call(bf16[128,2048]{1,0:T(8,128)(2,1)} %uh_in.1, bf16[128,2048]{1,0:T(8,128)(2,1)} %lh_in.1, ...), custom_call_target="tpu_custom_call" | custom-call | flops 28999999488 | bytes 30000000 | tf_op jit(solution)/shard_map/pallas_call | solution.py:554
  138.8 5.1 %shard_map.104 = (bf16[128,2048]{1,0:T(8,128)(2,1)}, bf16[128,2048]{1,0:T(8,128)(2,1)}, f32[2,256,2304]{2,1,0:T(8,128)}) custom-call(bf16[128,2048]{1,0:T(8,128)(2,1)} %get-tuple-element.9.up, bf16[128,2048]{1,0:T(8,128)(2,1)} %get-tuple-element.10.lo, bf16[256,2304]{1,0:T(8,128)(2,1)} %get-tuple-element.11.total, bf16[256,2304]{1,0:T(8,128)(2,1)} %get-tuple-element.12.own, ...), custom_call_target="tpu_custom_call" | custom-call | flops 3000000 | bytes 11500000 | tf_op jit(solution)/shard_map/pallas_call | solution.py:644
